TPU v7x, 512 devices: a whole 4x8x8 slice. The times are simulated.
512 devices in a mesh: replica: 16 (over x, z_lo), fsdp: 32 (over z_hi, y, core).
Axes of the slice: x: 4, y: 8, z: 8 (z_hi: 2, z_lo: 4; z = z_hi * 4 + z_lo), core: 2. Of those that a mesh axis runs over, the one named last changes fastest.
Arguments:
- activations: bfloat16 [16, 4096, 8192], P('replica', 'fsdp'), as said below
- norm_gain: float32 [16, 8192], P('replica'), may hold values from 0.1 to 1.9
- key_weight: bfloat16 [16, 8192, 512], P('replica', 'fsdp'), may hold values from -0.0625 to 0.0625
- key_cotangent: bfloat16 [16, 4096, 512], P('replica', 'fsdp'), as said below
- fragment_local: bfloat16 [16, 8192, 512], P('replica', 'fsdp'), may hold values from -6 to 6
- outer_params: float32 [8192, 512], P(('fsdp', 'replica')), may hold values from -6 to 6
- outer_momentum: float32 [8192, 512], P(('fsdp', 'replica')), may hold values from -3 to 3
Outputs:
- keys: bfloat16 [16, 4096, 512], P('replica', 'fsdp')
- weight_grad: bfloat16 [16, 8192, 512], P('replica', 'fsdp')
- gain_grad: float32 [16, 8192], P('replica')
- new_params: float32 [8192, 512], P(('fsdp', 'replica'))
- new_momentum: float32 [8192, 512], P(('fsdp', 'replica'))
Inputs may be any that keep to these rules, and one draw needn't show every extreme that they name: `activations`: independent entries; rows have scales of 1 to 16 and feature columns scales of 1 to 10. `key_cotangent`: independent entries whose scale varies with the token.
All inputs are finite; a program needn't handle non-finite values.
Results may differ from a plain program's by a relative error of at most 0.0049.
Values may be sent and summed in bfloat16 or wider, within the bound.
No kernel may reach another device: no remote copies, remote signals or barrier semaphores. Data moves between devices by JAX's collectives and lax.ppermute only.
A program may use at most 64 MiB of HBM per device.

v0:
```python
import jax
import jax.numpy as jnp
from jax import lax
from jax.sharding import PartitionSpec as P

epsilon = 1e-05


def body(
    activations, norm_gain, key_weight, key_cotangent, fragment_local, outer_params, outer_momentum
):
    values = activations[0].astype(jnp.float32)
    inverse = lax.rsqrt(jnp.mean(values * values, axis=1, keepdims=True) + epsilon)
    normed = values * inverse
    hidden = (normed * norm_gain[0][None, :]).astype(jnp.bfloat16)
    upstream = key_cotangent[0]
    weight_rows = key_weight[0]
    gathered = lax.all_gather(weight_rows, "fsdp", axis=0, tiled=True)
    key_values = jnp.dot(hidden, gathered, preferred_element_type=jnp.float32)
    hidden_grad = lax.dot_general(
        upstream, gathered, (((1,), (1,)), ((), ())), preferred_element_type=jnp.float32
    )
    gain_term = jnp.sum(hidden_grad * normed, axis=0)
    gain_total = lax.psum(gain_term, "fsdp")
    columns = lax.all_to_all(hidden, "fsdp", split_axis=1, concat_axis=0, tiled=True)
    grad_rows = lax.dot_general(
        columns,
        lax.all_gather(upstream, "fsdp", axis=0, tiled=True),
        (((0,), (0,)), ((), ())),
        preferred_element_type=jnp.float32,
    )
    local_rows = fragment_local[0].astype(jnp.float32)
    replicas = lax.axis_size("replica")
    share_rows = outer_params.shape[0]
    summed = lax.psum(local_rows, "replica")
    own_share = lax.dynamic_slice_in_dim(
        summed, lax.axis_index("replica") * share_rows, share_rows, 0
    )
    pseudo_grad = outer_params - own_share / replicas
    new_momentum = 0.9 * outer_momentum + pseudo_grad
    new_params = outer_params - 0.7 * (pseudo_grad + 0.9 * new_momentum)
    key_out = key_values.astype(jnp.bfloat16)[None]
    grad_out = grad_rows.astype(jnp.bfloat16)[None]
    return (key_out, grad_out, gain_total[None], new_params, new_momentum)


def solution(mesh):
    placed = (
        P("replica", "fsdp", None),
        P("replica", None),
        P("replica", "fsdp", None),
        P("replica", "fsdp", None),
        P("replica", "fsdp", None),
        P(("fsdp", "replica"), None),
        P(("fsdp", "replica"), None),
    )
    return jax.shard_map(
        body,
        mesh=mesh,
        in_specs=placed,
        out_specs=(
            P("replica", "fsdp", None),
            P("replica", "fsdp", None),
            P("replica", None),
            P(("fsdp", "replica"), None),
            P(("fsdp", "replica"), None),
        ),
        check_vma=False,
    )
```

profile of v0, /device:TPU:1, one launch (start us, length us, event | category | flops | bytes accessed | tf_op | source)
XLA Modules:
  0.0 471.2 jit_solution(12738543810220305159)
XLA Ops:
  8.0 0.0 copy-start
  8.0 0.0 copy-start.4
  8.0 0.0 all-reduce.2.cloned.1.call-start
  8.1 2.0 bitcast_convert_fusion
  10.0 0.0 all-reduce.2.cloned.1.call-update
  10.0 0.0 all-gather.7.cloned.1.call-start
  10.1 0.5 all-gather.7.cloned.1.call-update
  10.6 0.0 all-gather.5.cloned.1.call-start
  10.7 0.5 all-gather.5.cloned.1.call-update
  11.2 4.2 copy.13
  15.4 0.5 broadcast.27
  15.9 0.0 copy-done.4
  15.9 0.7 reduce.3
  16.7 0.0 copy-done
  16.7 0.5 fusion.5
  17.2 0.0 copy-start.2
  17.2 0.0 copy-start.3
  17.2 6.1 %fusion.7 = bf16[128,32,256]{2,0,1:T(8,128)(2,1)} fusion(f32[128,32,256]{2,1,0:T(8,128)} %bitcast.54, f32[32,256]{1,0:T(8,128)S(1)} %mul.59, f32[128]{0:T(128)S(1)} %add_rsqrt_fusion), kind=kLoop, calls=%fused_computation.11 | loop fusion | flops 3145728 | bytes 6324736 | tf_op jit(solution)/shard_map/convert_element_type | solution.py:15
  23.3 17.3 %all-to-all-start = ((bf16[128,32,256]{2,0,1:T(8,128)(2,1)}), bf16[128,32,256]{2,0,1:T(8,128)(2,1)}, u32[]{:S(2)}, u32[]{:S(2)}) async-start(bf16[128,32,256]{2,0,1:T(8,128)(2,1)} %fusion.7), calls=%async_computation | async-start | bytes 4194304 | tf_op jit(solution)/shard_map/all_to_all | solution.py:25
  40.6 236.9 %all-reduce.2.cloned.1.call-done = f32[256,512]{1,0:T(8,128)} async-done(((f32[256,512]{1,0:T(8,128)}), f32[256,512]{1,0:T(8,128)}) %all-reduce.2.cloned.1.call-update) | async-done | bytes 524304 | tf_op jit(solution)/shard_map/psum | solution.py:35
  277.5 0.0 copy-done.2
  277.5 0.0 copy-done.3
  277.5 1.4 multiply_subtract_fusion
  278.9 0.0 copy-start.1
  278.9 0.0 all-to-all-done
  278.9 0.0 all-gather.7.cloned.1.call-done
  278.9 4.8 %fusion.16 = bf16[1,256,512]{2,1,0:T(8,128)(2,1)} fusion(bf16[4096,256]{1,0:T(8,128)(2,1)} %bitcast.5, bf16[1,4096,512]{2,1,0:T(8,128)(2,1)} %all-gather.7.cloned.1.call-done), kind=kOutput, calls=%fused_computation.17 | convolution fusion | flops 1073872896 | bytes 6553600 | tf_op jit(solution)/shard_map/dot_general | solution.py:26
  283.7 0.0 all-gather.5.cloned.1.call-done
  283.7 0.0 copy-done.1
  283.7 6.3 %fusion.10 = f32[8192]{0:T(1024)S(1)} fusion(f32[128]{0:T(128)S(1)} %add_rsqrt_fusion, bf16[1,128,8192]{2,1,0:T(8,128)(2,1)S(1)} %copy-done, bf16[1,8192,512]{2,1,0:T(8,128)(2,1)} %all-gather.5.cloned.1.call-done, bf16[1,128,512]{2,1,0:T(8,128)(2,1)S(1)} %copy-done.1), kind=kOutput, calls=%fused_computation.15 | convolution fusion | flops 1077927936 | bytes 10650112 | tf_op jit(solution)/shard_map/dot_general | solution.py:20
  290.0 168.4 %psum.14 = f32[1,8192]{1,0:T(1,128)} all-reduce(f32[1,8192]{1,0:T(1,128)S(1)} %bitcast.57), channel_id=1, replica_groups=mesh['replica'=16,'fsdp'=32] {'fsdp'}, use_global_device_ids=true, to_apply=%region_2.0 | all-reduce | flops 8192 | bytes 65536 | tf_op jit(solution)/shard_map/psum | solution.py:24
  458.4 5.3 %fusion.22 = bf16[1,128,512]{2,1,0:T(8,128)(2,1)} fusion(bf16[1,8192,512]{2,1,0:T(8,128)(2,1)} %all-gather.5.cloned.1.call-done, bf16[1,128,8192]{2,1,0:T(8,128)(2,1)S(1)} %copy-done, f32[8192]{0:T(1024)S(1)} %bitcast.56, f32[128]{0:T(128)S(1)} %add_rsqrt_fusion), kind=kOutput, calls=%fused_computation.19 | convolution fusion | flops 1078001664 | bytes 10650112 | tf_op jit(solution)/shard_map/dot_general | solution.py:19
  (2 shorter events, 0.0 us)
Async XLA Ops:
  8.0 8.7 %copy-start = (bf16[1,128,8192]{2,1,0:T(8,128)(2,1)S(1)}, bf16[1,128,8192]{2,1,0:T(8,128)(2,1)}, u32[]{:S(2)}) copy-start(bf16[1,128,8192]{2,1,0:T(8,128)(2,1)} %param.7) | copy-start | bytes 6291460
  8.0 7.9 %copy-start.4 = (f32[1,8192]{1,0:T(1,128)S(1)}, f32[1,8192]{1,0:T(1,128)}, u32[]{:S(2)}) copy-start(f32[1,8192]{1,0:T(1,128)} %param.8) | copy-start | bytes 98308
  8.0 269.5 %all-reduce.2.cloned.1.call-start = ((), (), s32[]{:S(2)}) async-start(), calls=%async_computation.1 | async-start | bytes 1048576 | tf_op jit(solution)/shard_map/psum | solution.py:35
  10.0 268.9 %all-gather.7.cloned.1.call-start = ((), (), s32[]{:S(2)}) async-start(), calls=%async_computation.3 | async-start | bytes 4325376 | tf_op jit(solution)/shard_map/all_gather | solution.py:28
  10.6 273.1 %all-gather.5.cloned.1.call-start = ((), (), s32[]{:S(2)}) async-start(), calls=%async_computation.2 | async-start | bytes 8650752 | tf_op jit(solution)/shard_map/all_gather | solution.py:18
  17.2 260.3 %copy-start.2 = (f32[16,512]{1,0:T(8,128)S(1)}, f32[16,512]{1,0:T(8,128)}, u32[]{:S(2)}) copy-start(f32[16,512]{1,0:T(8,128)} %param.12) | copy-start | bytes 98308
  17.2 260.3 %copy-start.3 = (f32[16,512]{1,0:T(8,128)S(1)}, f32[16,512]{1,0:T(8,128)}, u32[]{:S(2)}) copy-start(f32[16,512]{1,0:T(8,128)} %param.13) | copy-start | bytes 98308
  23.3 255.6 %all-to-all-start = ((bf16[128,32,256]{2,0,1:T(8,128)(2,1)}), bf16[128,32,256]{2,0,1:T(8,128)(2,1)}, u32[]{:S(2)}, u32[]{:S(2)}) async-start(bf16[128,32,256]{2,0,1:T(8,128)(2,1)} %fusion.7), calls=%async_computation | async-start | bytes 4194304 | tf_op jit(solution)/shard_map/all_to_all | solution.py:25
  278.9 4.9 %copy-start.1 = (bf16[1,128,512]{2,1,0:T(8,128)(2,1)S(1)}, bf16[1,128,512]{2,1,0:T(8,128)(2,1)}, u32[]{:S(2)}) copy-start(bf16[1,128,512]{2,1,0:T(8,128)(2,1)} %param.10) | copy-start | bytes 393220
Sparse Core Ops, SparseCore 0:
  11.8 265.6 all-reduce.1
Sparse Core Ops, SparseCore 1:
  13.9 130.1 all-gather.6
  147.2 130.2 all-gather.4
where the time goes:
time: 479 us; the launch traced here: 471 us
  waiting for transfers between devices  238 us (50%)
  blocking collectives  168 us (35%)
  starting transfers between devices  17.4 us (4%)
  matrix products  16.5 us (3%)
  between operations  15.6 us (3%)
  other arithmetic  10.7 us (2%)
    psum x1, waiting for transfers between devices, body(): summed = lax.psum(local_rows, 'replica')  237 us
    psum x1, blocking collectives, body(): gain_total = lax.psum(gain_term, 'fsdp')  168 us
    all_to_all x1, starting transfers between devices, body(): lax.all_to_all(hidden, 'fsdp', split_axis=1, concat_axis=0, tiled=True)  17.3 us
  transfers between devices with their start and end apart: 4, of which 1 were waited for; matrix products, arithmetic and copies ran while one was open for 4% of the time, Pallas kernels for 0%

commit v1 on v0

--- a/solution.py
+++ b/solution.py
@@ -15,33 +15,38 @@
     hidden = (normed * norm_gain[0][None, :]).astype(jnp.bfloat16)
     upstream = key_cotangent[0]
     weight_rows = key_weight[0]
+    groups = lax.axis_size("fsdp")
+    rows = weight_rows.shape[0]
+    columns = lax.all_to_all(hidden, "fsdp", split_axis=1, concat_axis=0, tiled=True)
+    all_upstream = lax.all_gather(upstream, "fsdp", axis=0, tiled=True)
     gathered = lax.all_gather(weight_rows, "fsdp", axis=0, tiled=True)
-    key_values = jnp.dot(hidden, gathered, preferred_element_type=jnp.float32)
-    hidden_grad = lax.dot_general(
-        upstream, gathered, (((1,), (1,)), ((), ())), preferred_element_type=jnp.float32
+
+    pieces = lax.all_to_all(
+        fragment_local[0], "replica", split_axis=0, concat_axis=0, tiled=True
     )
-    gain_term = jnp.sum(hidden_grad * normed, axis=0)
-    gain_total = lax.psum(gain_term, "fsdp")
-    columns = lax.all_to_all(hidden, "fsdp", split_axis=1, concat_axis=0, tiled=True)
-    grad_rows = lax.dot_general(
-        columns,
-        lax.all_gather(upstream, "fsdp", axis=0, tiled=True),
-        (((0,), (0,)), ((), ())),
-        preferred_element_type=jnp.float32,
-    )
-    local_rows = fragment_local[0].astype(jnp.float32)
     replicas = lax.axis_size("replica")
     share_rows = outer_params.shape[0]
-    summed = lax.psum(local_rows, "replica")
-    own_share = lax.dynamic_slice_in_dim(
-        summed, lax.axis_index("replica") * share_rows, share_rows, 0
+    own_share = jnp.sum(
+        pieces.reshape(replicas, share_rows, -1).astype(jnp.float32), axis=0
     )
     pseudo_grad = outer_params - own_share / replicas
     new_momentum = 0.9 * outer_momentum + pseudo_grad
     new_params = outer_params - 0.7 * (pseudo_grad + 0.9 * new_momentum)
+
+    grad_rows = lax.dot_general(
+        columns, all_upstream, (((0,), (0,)), ((), ())), preferred_element_type=jnp.float32
+    )
+    own_gain = lax.dynamic_slice_in_dim(
+        norm_gain[0], lax.axis_index("fsdp") * rows, rows, 0
+    )
+    own_terms = jnp.sum(grad_rows * weight_rows.astype(jnp.float32), axis=1) / own_gain
+    gain_total = lax.all_to_all(
+        jnp.broadcast_to(own_terms[None], (groups, rows)), "fsdp", 0, 0, tiled=True
+    ).reshape(1, groups * rows)
+    key_values = jnp.dot(hidden, gathered, preferred_element_type=jnp.float32)
     key_out = key_values.astype(jnp.bfloat16)[None]
     grad_out = grad_rows.astype(jnp.bfloat16)[None]
-    return (key_out, grad_out, gain_total[None], new_params, new_momentum)
+    return (key_out, grad_out, gain_total, new_params, new_momentum)
 
 
 def solution(mesh):

time: 479 us -> 294 us (0.61); the launches traced: 471 us -> 293 us
  blocking collectives: 168 us -> 0 us
  waiting for transfers between devices: 238 us -> 220 us
  starting transfers between devices: 17.4 us -> 33.3 us
  other arithmetic: 10.7 us -> 4.73 us
    psum x1 -> x0, waiting for transfers between devices: 237 us -> none  [body(): summed = lax.psum(local_rows, 'replica')]
    psum x1 -> x0, blocking collectives: 168 us -> none  [body(): gain_total = lax.psum(gain_term, 'fsdp')]
    all_gather x1, waiting for transfers between devices: 0.01 us -> 109 us  [body(): gathered = lax.all_gather(weight_rows, 'fsdp', axis=0, tiled=True)]
    all_to_all x1, waiting for transfers between devices: 0.01 us -> 57.6 us  [body(): lax.all_to_all(hidden, 'fsdp', split_axis=1, concat_axis=0, tiled=True)]
    all_gather x1, waiting for transfers between devices: 0.01 us -> 38.2 us  [body(): all_upstream = lax.all_gather(upstream, 'fsdp', axis=0, tiled=True)]
    all_to_all x0 -> x2, starting transfers between devices: none -> 18 us  [the longest x1 10.4 us: body(): lax.all_to_all(fragment_local[0], 'replica', split_axis=0, concat_axis=0,...]
    all_to_all x0 -> x2, waiting for transfers between devices: none -> 13.1 us  [the longest x1 11.2 us: body(): lax.all_to_all(jnp.broadcast_to(own_terms[None], (groups, rows)), 'fsdp',...]
    dot_general x2 -> x1, matrix products: 11.1 us -> 4.8 us  [body(): lax.dot_general(columns, all_upstream, (((0,), (0,)), ((), ())), preferre...]
  transfers between devices with their start and end apart: 4 -> 5, of which waited for: 1 -> 5; matrix products, arithmetic and copies ran while one was open for 4% -> 6% of each run, Pallas kernels for 0% -> 0%
where the time goes in v1:
time: 294 us; the launch traced here: 293 us
  waiting for transfers between devices  220 us (75%)
  starting transfers between devices  33.3 us (11%)
  between operations  14.1 us (5%)
  matrix products  12.3 us (4%)
  local copies, waits for them, and re-layouts  9.11 us (3%)
  other arithmetic  4.73 us (2%)
    all_gather x1, waiting for transfers between devices, body(): gathered = lax.all_gather(weight_rows, 'fsdp', axis=0, tiled=True)  109 us
    all_to_all x1, waiting for transfers between devices, body(): lax.all_to_all(hidden, 'fsdp', split_axis=1, concat_axis=0, tiled=True)  57.6 us
    all_gather x1, waiting for transfers between devices, body(): all_upstream = lax.all_gather(upstream, 'fsdp', axis=0, tiled=True)  38.2 us
    all_to_all x1, starting transfers between devices, body(): lax.all_to_all(hidden, 'fsdp', split_axis=1, concat_axis=0, tiled=True)  15.2 us
    all_to_all x1, waiting for transfers between devices, body(): lax.all_to_all(jnp.broadcast_to(own_terms[None], (groups, rows)), 'fsdp',...  11.2 us
    all_to_all x1, starting transfers between devices, body(): lax.all_to_all(fragment_local[0], 'replica', split_axis=0, concat_axis=0,...  10.4 us
    all_to_all x1, starting transfers between devices, body(): lax.all_to_all(jnp.broadcast_to(own_terms[None], (groups, rows)), 'fsdp',...  7.64 us
    dot_general x1, matrix products, body(): key_values = jnp.dot(hidden, gathered, preferred_element_type=jnp.float32)  7.47 us
  transfers between devices with their start and end apart: 5, of which 5 were waited for; matrix products, arithmetic and copies ran while one was open for 6% of the time, Pallas kernels for 0%

profile of v1, /device:TPU:1, one launch (start us, length us, event | category | flops | bytes accessed | tf_op | source)
XLA Modules:
  0.0 293.1 jit_solution(9677103709520319485)
XLA Ops:
  7.2 0.0 copy-start.1
  7.2 0.0 all-gather.7.cloned.1.call-start
  7.2 0.7 all-gather.7.cloned.1.call-update
  7.9 0.0 all-gather.5.cloned.1.call-start
  8.0 0.7 all-gather.5.cloned.1.call-update
  8.7 10.4 %all-to-all-start.2 = ((bf16[16,16,512]{2,1,0:T(8,128)(2,1)}), bf16[16,16,512]{2,1,0:T(8,128)(2,1)S(1)}, u32[]{:S(2)}, u32[]{:S(2)}) async-start(bf16[16,16,512]{2,1,0:T(8,128)(2,1)} %bitcast.45), calls=%async_computation.2 | async-start | bytes 524288 | tf_op jit(solution)/shard_map/all_to_all | solution.py:24
  19.1 3.2 %copy.14 = bf16[1,128,8192]{1,2,0:T(8,128)(2,1)S(1)} copy(bf16[1,128,8192]{2,1,0:T(8,128)(2,1)} %param.7) | data formatting | bytes 4194304 | tf_op args[0]
  22.3 0.5 broadcast.31
  22.8 0.0 copy-done.1
  22.8 0.7 reduce.3
  23.6 1.1 fusion.4
  24.7 2.2 multiply_convert_fusion
  26.9 0.0 copy-start
  26.9 1.9 all-to-all-done.2
  28.7 15.2 %all-to-all-start = ((bf16[128,32,256]{0,2,1:T(8,128)(2,1)}), bf16[128,32,256]{0,2,1:T(8,128)(2,1)}, u32[]{:S(2)}, u32[]{:S(2)}) async-start(bf16[128,32,256]{0,2,1:T(8,128)(2,1)} %multiply_convert_fusion), calls=%async_computation | async-start | bytes 4194304 | tf_op jit(solution)/shard_map/all_to_all | solution.py:20
  44.0 57.6 %all-to-all-done = bf16[128,32,256]{0,2,1:T(8,128)(2,1)} async-done(((bf16[128,32,256]{0,2,1:T(8,128)(2,1)}), bf16[128,32,256]{0,2,1:T(8,128)(2,1)}, u32[]{:S(2)}, u32[]{:S(2)}) %all-to-all-start) | async-done | bytes 2097184 | tf_op jit(solution)/shard_map/all_to_all | solution.py:20
  101.6 4.1 %copy.15 = bf16[32,128,256]{2,1,0:T(8,128)(2,1)} copy(bf16[32,128,256]{1,2,0:T(8,128)(2,1)} %bitcast.5) | data formatting | bytes 4194304 | tf_op jit(solution)/shard_map/all_to_all | solution.py:20
  105.7 38.2 %all-gather.7.cloned.1.call-done = bf16[1,4096,512]{2,1,0:T(8,128)(2,1)} async-done(((bf16[1,128,512]{2,1,0:T(8,128)(2,1)}), bf16[1,4096,512]{2,1,0:T(8,128)(2,1)}) %all-gather.7.cloned.1.call-update) | async-done | bytes 4194320 | tf_op jit(solution)/shard_map/all_gather | solution.py:21
  144.0 0.0 copy-done
  144.0 0.0 copy-start.2
  144.0 0.0 copy-start.3
  144.0 4.8 %fusion.21 = (f32[256]{0:T(256)S(1)}, bf16[1,256,512]{2,1,0:T(8,128)(2,1)}) fusion(bf16[1,256,512]{2,1,0:T(8,128)(2,1)S(1)} %copy-done, bf16[4096,256]{1,0:T(8,128)(2,1)} %bitcast.44, bf16[1,4096,512]{2,1,0:T(8,128)(2,1)} %all-gather.7.cloned.1.call-done), kind=kOutput, calls=%fused_computation.16 | convolution fusion | flops 1074265856 | bytes 6816768 | tf_op jit(solution)/shard_map/dot_general | solution.py:36
  148.8 0.6 broadcast_in_dim.15
  149.4 7.6 %all-to-all-start.1 = ((f32[32,1,256]{2,1,0:T(1,128)}), f32[32,1,256]{2,1,0:T(1,128)S(1)}, u32[]{:S(2)}, u32[]{:S(2)}) async-start(f32[32,1,256]{2,1,0:T(1,128)} %broadcast_in_dim.15), calls=%async_computation.1 | async-start | bytes 65536 | tf_op jit(solution)/shard_map/all_to_all | solution.py:43
  157.1 0.0 copy-done.2
  157.1 0.0 copy-done.3
  157.1 0.6 multiply_subtract_fusion
  157.7 11.2 %all-to-all-done.1 = f32[32,1,256]{2,1,0:T(1,128)S(1)} async-done(((f32[32,1,256]{2,1,0:T(1,128)}), f32[32,1,256]{2,1,0:T(1,128)S(1)}, u32[]{:S(2)}, u32[]{:S(2)}) %all-to-all-start.1) | async-done | bytes 32800 | tf_op jit(solution)/shard_map/all_to_all | solution.py:43
  168.9 109.3 %all-gather.5.cloned.1.call-done = bf16[1,8192,512]{2,1,0:T(8,128)(2,1)} async-done(((bf16[1,256,512]{2,1,0:T(8,128)(2,1)}), bf16[1,8192,512]{2,1,0:T(8,128)(2,1)}) %all-gather.5.cloned.1.call-update) | async-done | bytes 8388624 | tf_op jit(solution)/shard_map/all_gather | solution.py:22
  278.2 7.5 %fusion.16 = bf16[1,128,512]{2,1,0:T(8,128)(2,1)} fusion(bf16[1,8192,512]{2,1,0:T(8,128)(2,1)} %all-gather.5.cloned.1.call-done, bf16[1,128,8192]{1,2,0:T(8,128)(2,1)S(1)} %copy.14, f32[8192]{0:T(1024)S(1)} %bitcast.46, f32[128]{0:T(128)S(1)} %add_rsqrt_fusion), kind=kOutput, calls=%fused_computation.14 | convolution fusion | flops 1078001664 | bytes 10650112 | tf_op jit(solution)/shard_map/dot_general | solution.py:46
  285.7 0.6 copy.17
  (4 shorter events, 0.1 us)
Async XLA Ops:
  7.2 15.6 %copy-start.1 = (f32[1,8192]{1,0:T(1,128)S(1)}, f32[1,8192]{1,0:T(1,128)}, u32[]{:S(2)}) copy-start(f32[1,8192]{1,0:T(1,128)} %param.8) | copy-start | bytes 98308
  7.2 136.8 %all-gather.7.cloned.1.call-start = ((), (), s32[]{:S(2)}) async-start(), calls=%async_computation.4 | async-start | bytes 4325376 | tf_op jit(solution)/shard_map/all_gather | solution.py:21
  7.9 270.3 %all-gather.5.cloned.1.call-start = ((), (), s32[]{:S(2)}) async-start(), calls=%async_computation.3 | async-start | bytes 8650752 | tf_op jit(solution)/shard_map/all_gather | solution.py:22
  8.7 20.1 %all-to-all-start.2 = ((bf16[16,16,512]{2,1,0:T(8,128)(2,1)}), bf16[16,16,512]{2,1,0:T(8,128)(2,1)S(1)}, u32[]{:S(2)}, u32[]{:S(2)}) async-start(bf16[16,16,512]{2,1,0:T(8,128)(2,1)} %bitcast.45), calls=%async_computation.2 | async-start | bytes 524288 | tf_op jit(solution)/shard_map/all_to_all | solution.py:24
  26.9 117.1 %copy-start = (bf16[1,256,512]{2,1,0:T(8,128)(2,1)S(1)}, bf16[1,256,512]{2,1,0:T(8,128)(2,1)}, u32[]{:S(2)}) copy-start(bf16[1,256,512]{2,1,0:T(8,128)(2,1)} %param.9) | copy-start | bytes 786436
  28.7 72.9 %all-to-all-start = ((bf16[128,32,256]{0,2,1:T(8,128)(2,1)}), bf16[128,32,256]{0,2,1:T(8,128)(2,1)}, u32[]{:S(2)}, u32[]{:S(2)}) async-start(bf16[128,32,256]{0,2,1:T(8,128)(2,1)} %multiply_convert_fusion), calls=%async_computation | async-start | bytes 4194304 | tf_op jit(solution)/shard_map/all_to_all | solution.py:20
  144.0 13.1 %copy-start.2 = (f32[16,512]{1,0:T(8,128)S(1)}, f32[16,512]{1,0:T(8,128)}, u32[]{:S(2)}) copy-start(f32[16,512]{1,0:T(8,128)} %param.12) | copy-start | bytes 98308
  144.0 13.1 %copy-start.3 = (f32[16,512]{1,0:T(8,128)S(1)}, f32[16,512]{1,0:T(8,128)}, u32[]{:S(2)}) copy-start(f32[16,512]{1,0:T(8,128)} %param.13) | copy-start | bytes 98308
  149.4 19.5 %all-to-all-start.1 = ((f32[32,1,256]{2,1,0:T(1,128)}), f32[32,1,256]{2,1,0:T(1,128)S(1)}, u32[]{:S(2)}, u32[]{:S(2)}) async-start(f32[32,1,256]{2,1,0:T(1,128)} %broadcast_in_dim.15), calls=%async_computation.1 | async-start | bytes 65536 | tf_op jit(solution)/shard_map/all_to_all | solution.py:43
Sparse Core Ops, SparseCore 0:
  11.3 132.5 all-gather.6
  147.3 130.8 all-gather.4

commit v2 on v0

v2 whole, which is shorter than its diff:
```python
import jax
import jax.numpy as jnp
from jax import lax
from jax.experimental import pallas as pl
from jax.experimental.pallas import tpu as pltpu
from jax.sharding import Mesh, PartitionSpec as P

epsilon = 1e-05
F32 = jnp.float32
BF16 = jnp.bfloat16
FSDP = ("z", "y", "core")


def norm_kernel(place, x_ref, gain_ref, out_ref):
    slots, _, width = out_ref.shape
    part = width // 4
    half = x_ref.shape[1] // 2
    values = x_ref[...].astype(F32)
    total = jnp.sum(values * values, axis=1, keepdims=True)
    inverse = lax.rsqrt(total / x_ref.shape[1] + epsilon)
    for slot in range(slots):
        for piece in range(4):
            z = place[0] ^ (piece & 1)
            core = place[1] ^ (piece >> 1)
            start = pl.multiple_of(z * half + slot * 2 * part + core * part, part)
            block = x_ref[:, pl.ds(start, part)].astype(F32)
            scale = gain_ref[:, pl.ds(start, part)]
            out_ref[slot, :, piece * part:(piece + 1) * part] = (
                (block * inverse) * scale
            ).astype(out_ref.dtype)


def norm(place, x, gain, slots):
    tokens, width = x.shape
    rows = 32
    return pl.pallas_call(
        norm_kernel,
        out_shape=jax.ShapeDtypeStruct((slots, tokens, width // slots), BF16),
        grid_spec=pltpu.PrefetchScalarGridSpec(
            num_scalar_prefetch=1,
            grid=(tokens // rows,),
            in_specs=[
                pl.BlockSpec((rows, width), lambda i, place: (i, 0)),
                pl.BlockSpec((1, width), lambda i, place: (0, 0)),
            ],
            out_specs=pl.BlockSpec((slots, rows, width // slots), lambda i, place: (0, i, 0)),
        ),
        compiler_params=pltpu.CompilerParams(vmem_limit_bytes=32 * 1024 * 1024),
        cost_estimate=pl.CostEstimate(
            flops=6 * tokens * width, bytes_accessed=4 * tokens * width, transcendentals=tokens
        ),
    )(place, x, gain)


def swap(x, axis):
    return lax.ppermute(x, axis, [(0, 1), (1, 0)])


def body(
    activations, norm_gain, key_weight, key_cotangent, fragment_local, outer_params, outer_momentum
):
    slots = lax.axis_size("y")
    z, core = lax.axis_index("z"), lax.axis_index("core")
    place = jnp.stack([z, core]).astype(jnp.int32)
    weight = key_weight[0]
    upstream = key_cotangent[0]
    part, keys = weight.shape
    tokens = upstream.shape[0]

    weight_two = jnp.concatenate([weight, swap(weight, "z")], axis=0)
    weight_slot = jnp.concatenate([weight_two, swap(weight_two, "core")], axis=0)

    hidden = norm(place, activations[0], norm_gain, slots)
    columns = lax.all_to_all(hidden, "y", 0, 0, tiled=True).reshape(slots * tokens, 4 * part)
    all_upstream = lax.all_gather(upstream, "y", axis=0, tiled=True)

    key_terms = jnp.dot(columns, weight_slot, preferred_element_type=F32).astype(BF16)
    key_parts = lax.all_to_all(key_terms, "y", 0, 0, tiled=True)
    key_out = jnp.sum(key_parts.reshape(slots, tokens, keys).astype(F32), axis=0).astype(BF16)

    contract = (((0,), (0,)), ((), ()))
    far = lax.dot_general(
        columns[:, 2 * part:], all_upstream, contract, preferred_element_type=F32
    )
    near = lax.dot_general(
        columns[:, :2 * part], all_upstream, contract, preferred_element_type=F32
    )
    chip = near + swap(far, "core")
    grad_rows = chip[:part] + swap(chip[part:].astype(BF16), "z").astype(F32)

    terms = jnp.concatenate(
        [
            jnp.sum(near * weight_slot[:2 * part].astype(F32), axis=1),
            jnp.sum(far * weight_slot[2 * part:].astype(F32), axis=1),
        ]
    )
    devices = 4 * slots
    spread = lax.all_to_all(
        jnp.broadcast_to(terms[None], (devices, 4 * part)), FSDP, 0, 0, tiled=True
    ).reshape(2, slots, 2, 2, 2, part)
    total = [
        [
            sum(
                spread[a, :, b, core_to ^ b, z_to ^ a]
                for a in range(2)
                for b in range(2)
            )
            for core_to in range(2)
        ]
        for z_to in range(2)
    ]
    gain_total = jnp.stack([jnp.stack(t, axis=1) for t in total]).reshape(1, -1) / norm_gain

    pieces = lax.all_to_all(fragment_local[0], "replica", 0, 0, tiled=True)
    replicas = lax.axis_size("replica")
    own_share = jnp.sum(
        pieces.reshape(replicas, outer_params.shape[0], -1).astype(F32), axis=0
    )
    pseudo_grad = outer_params - own_share / replicas
    new_momentum = 0.9 * outer_momentum + pseudo_grad
    new_params = outer_params - 0.7 * (pseudo_grad + 0.9 * new_momentum)
    return (key_out[None], grad_rows.astype(BF16)[None], gain_total, new_params, new_momentum)


def solution(mesh):
    shape = mesh.devices.shape
    split = Mesh(
        mesh.devices.reshape(shape[0], 2, shape[1] // 4, 2), ("replica",) + FSDP
    )
    rows = P("replica", FSDP, None)
    share = P(FSDP + ("replica",), None)
    return jax.shard_map(
        body,
        mesh=split,
        in_specs=(rows, P("replica", None), rows, rows, rows, share, share),
        out_specs=(rows, rows, P("replica", None), share, share),
        check_vma=False,
    )
```

time: 479 us -> 172 us (0.36); the launches traced: 471 us -> 171 us
  blocking collectives: 168 us -> 0 us
  waiting for transfers between devices: 238 us -> 81.4 us
  starting transfers between devices: 17.4 us -> 56.9 us
  matrix products: 16.5 us -> 8.55 us
  other arithmetic: 10.7 us -> 2.8 us
    psum x1 -> x0, waiting for transfers between devices: 237 us -> none  [body(): summed = lax.psum(local_rows, 'replica')]
    psum x1 -> x0, blocking collectives: 168 us -> none  [body(): gain_total = lax.psum(gain_term, 'fsdp')]
    all_gather x2 -> x1, waiting for transfers between devices: 0.01 us -> 32.2 us  [body(): all_upstream = lax.all_gather(upstream, 'y', axis=0, tiled=True)]
    all_to_all x1 -> x4, waiting for transfers between devices: 0.01 us -> 30 us  [the longest x1 12.4 us: body(): key_parts = lax.all_to_all(key_terms, 'y', 0, 0, tiled=True)]
    ppermute x0 -> x4, starting transfers between devices: none -> 24.3 us  [swap(): return lax.ppermute(x, axis, [(0, 1), (1, 0)])]
    ppermute x0 -> x4, waiting for transfers between devices: none -> 18.5 us  [swap(): return lax.ppermute(x, axis, [(0, 1), (1, 0)])]
    all_to_all x1 -> x4, starting transfers between devices: 17.3 us -> 32.5 us  [the longest x1 12.3 us: body(): lax.all_to_all(jnp.broadcast_to(terms[None], (devices, 4 * part)), FSDP,...]
    convert_element_type x2 -> x0, other arithmetic: 8.05 us -> none  [the longest x1 6.1 us: body(): hidden = (normed * norm_gain[0][None, :]).astype(jnp.bfloat16)]
  transfers between devices with their start and end apart: 4 -> 9, of which waited for: 1 -> 8; matrix products, arithmetic and copies ran while one was open for 4% -> 5% of each run, Pallas kernels for 0% -> 0%
where the time goes in v2:
time: 172 us; the launch traced here: 171 us
  waiting for transfers between devices  81.4 us (47%)
  starting transfers between devices  56.9 us (33%)
  between operations  14.2 us (8%)
  matrix products  8.55 us (5%)
  local copies, waits for them, and re-layouts  4.26 us (2%)
  Pallas kernels  3.1 us (2%)
  other arithmetic  2.8 us (2%)
    all_gather x1, waiting for transfers between devices, body(): all_upstream = lax.all_gather(upstream, 'y', axis=0, tiled=True)  32.2 us
    ppermute x4, starting transfers between devices, swap(): return lax.ppermute(x, axis, [(0, 1), (1, 0)])  24.3 us
    ppermute x4, waiting for transfers between devices, swap(): return lax.ppermute(x, axis, [(0, 1), (1, 0)])  18.5 us
    all_to_all x1, waiting for transfers between devices, body(): key_parts = lax.all_to_all(key_terms, 'y', 0, 0, tiled=True)  12.4 us
    all_to_all x1, starting transfers between devices, body(): lax.all_to_all(jnp.broadcast_to(terms[None], (devices, 4 * part)), FSDP,...  12.3 us
    all_to_all x1, waiting for transfers between devices, body(): lax.all_to_all(jnp.broadcast_to(terms[None], (devices, 4 * part)), FSDP,...  10.7 us
    all_to_all x1, starting transfers between devices, body(): pieces = lax.all_to_all(fragment_local[0], 'replica', 0, 0, tiled=True)  8.92 us
    all_to_all x1, starting transfers between devices, body(): lax.all_to_all(hidden, 'y', 0, 0, tiled=True)  7.78 us
  transfers between devices with their start and end apart: 9, of which 8 were waited for; matrix products, arithmetic and copies ran while one was open for 5% of the time, Pallas kernels for 0%

profile of v2, /device:TPU:1, one launch (start us, length us, event | category | flops | bytes accessed | tf_op | source)
XLA Modules:
  0.0 171.2 jit_solution(9005676481437711504)
XLA Ops:
  7.2 0.1 pad_add_fusion.place
  7.2 1.6 copy-done
  8.8 0.8 copy-done.1
  9.6 3.1 %shard_map.110 = bf16[8,128,1024]{2,1,0:T(8,128)(2,1)} custom-call(s32[2]{0:T(128)S(1)} %pad_add_fusion.place, bf16[128,8192]{1,0:T(8,128)(2,1)S(1)} %bitcast.98, f32[1,8192]{1,0:T(1,128)S(1)} %copy-done.1), custom_call_target="tpu_custom_call" | custom-call | flops 6291456 | bytes 4194304 | tf_op jit(solution)/shard_map/pallas_call | solution.py:36
  12.7 7.8 %all-to-all-start = ((bf16[8,128,1024]{2,1,0:T(8,128)(2,1)}), bf16[8,128,1024]{2,1,0:T(8,128)(2,1)S(1)}, u32[]{:S(2)}, u32[]{:S(2)}) async-start(bf16[8,128,1024]{2,1,0:T(8,128)(2,1)} %shard_map.110), calls=%async_computation | async-start | bytes 4194304 | tf_op jit(solution)/shard_map/all_to_all | solution.py:74
  20.5 0.7 all-gather.3.cloned.1.call-update
  21.2 0.1 copy.28
  21.4 10.6 %collective-permute-start = (bf16[256,512]{0,1:T(8,128)(2,1)S(1)}, bf16[256,512]{0,1:T(8,128)(2,1)S(1)}, u32[]{:S(2)}, u32[]{:S(2)}) collective-permute-start(bf16[256,512]{0,1:T(8,128)(2,1)S(1)} %bitcast.102), channel_id=1, source_target_pairs={{0,16},{16,0},{1,17},{17,1},{2,18},{18,2},{3,19},{19,3},{4,20},{20... | collective-permute-start | bytes 786440 | tf_op jit(solution)/shard_map/ppermute | solution.py:56
  32.0 5.7 %collective-permute-done = bf16[256,512]{0,1:T(8,128)(2,1)S(1)} collective-permute-done((bf16[256,512]{0,1:T(8,128)(2,1)S(1)}, bf16[256,512]{0,1:T(8,128)(2,1)S(1)}, u32[]{:S(2)}, u32[]{:S(2)}) %collective-permute-start) | collective-permute-done | bytes 262176 | tf_op jit(solution)/shard_map/ppermute | solution.py:56
  37.7 8.3 %collective-permute-start.1 = (bf16[512,512]{0,1:T(8,128)(2,1)S(1)}, bf16[512,512]{0,1:T(8,128)(2,1)S(1)}, u32[]{:S(2)}, u32[]{:S(2)}) collective-permute-start(bf16[512,512]{0,1:T(8,128)(2,1)S(1)} %pad_maximum_fusion), channel_id=1, source_target_pairs={{0,1},{1,0},{2,3},{3,2},{4,5},{5,4},{6,7},{7,6},{8,9},{9,8},{10,11... | collective-permute-start | bytes 1572872 | tf_op jit(solution)/shard_map/ppermute | solution.py:56
  46.1 1.5 collective-permute-done.1
  47.6 32.2 %all-gather.3.cloned.1.call-done = bf16[1,1024,512]{2,1,0:T(8,128)(2,1)} async-done(((bf16[1,128,512]{2,1,0:T(8,128)(2,1)}), bf16[1,1024,512]{2,1,0:T(8,128)(2,1)}) %all-gather.3.cloned.1.call-update) | async-done | bytes 1048592 | tf_op jit(solution)/shard_map/all_gather | solution.py:75
  79.9 3.0 %multiply_reduce_fusion = (f32[512]{0:T(512)S(1)}, f32[512,512]{0,1:T(8,128)}) fusion(bf16[512,512]{0,1:T(8,128)(2,1)S(1)} %collective-permute-done.1, bf16[1,1024,512]{2,1,0:T(8,128)(2,1)} %all-gather.3.cloned.1.call-done, bf16[1024,1024]{1,0:T(8,128)(2,1)S(1)} %bitcast.99), kind=kOutput, calls=%fused_computation.12 | convolution fusion | flops 537656832 | bytes 3672064 | tf_op jit(solution)/shard_map/dot_general | solution.py:82
  82.9 3.0 %collective-permute-start.2 = (f32[512,512]{0,1:T(8,128)}, f32[512,512]{0,1:T(8,128)}, u32[]{:S(2)}, u32[]{:S(2)}) collective-permute-start(f32[512,512]{0,1:T(8,128)} %get-tuple-element.29), channel_id=1, source_target_pairs={{0,1},{1,0},{2,3},{3,2},{4,5},{5,4},{6,7},{7,6},{8,9},{9,8},{10,11... | collective-permute-start | bytes 3145736 | tf_op jit(solution)/shard_map/ppermute | solution.py:56
  85.9 8.9 %all-to-all-start.3 = ((bf16[16,16,512]{2,1,0:T(8,128)(2,1)}), bf16[16,16,512]{2,1,0:T(8,128)(2,1)S(1)}, u32[]{:S(2)}, u32[]{:S(2)}) async-start(bf16[16,16,512]{2,1,0:T(8,128)(2,1)} %bitcast.15), calls=%async_computation.3 | async-start | bytes 524288 | tf_op jit(solution)/shard_map/all_to_all | solution.py:114
  94.8 3.3 %multiply_reduce_fusion.1 = (f32[512]{0:T(512)S(1)}, f32[512,512]{0,1:T(8,128)}) fusion(bf16[256,512]{0,1:T(8,128)(2,1)S(1)} %collective-permute-done, bf16[256,512]{0,1:T(8,128)(2,1)S(1)} %bitcast.104, f32[512,512]{0,1:T(8,128)} %collective-permute-done.2, bf16[1,1024,512]{2,1,0:T(8,128)(2,1)} %all-gather.3.cloned.1.call-done, ...), kind=kOutput, calls=%fused_computation.13 | convolution fusion | flops 538705408 | bytes 4720640 | tf_op jit(solution)/shard_map/dot_general | solution.py:85
  98.1 6.8 %all-to-all-done.3 = bf16[16,16,512]{2,1,0:T(8,128)(2,1)S(1)} async-done(((bf16[16,16,512]{2,1,0:T(8,128)(2,1)}), bf16[16,16,512]{2,1,0:T(8,128)(2,1)S(1)}, u32[]{:S(2)}, u32[]{:S(2)}) %all-to-all-start.3) | async-done | bytes 262176 | tf_op jit(solution)/shard_map/all_to_all | solution.py:114
  104.9 0.7 broadcast_in_dim.14
  105.6 12.3 %all-to-all-start.2 = ((f32[32,1,1024]{2,1,0:T(1,128)}), f32[32,1,1024]{2,1,0:T(1,128)S(1)}, u32[]{:S(2)}, u32[]{:S(2)}) async-start(f32[32,1,1024]{2,1,0:T(1,128)} %broadcast_in_dim.14), calls=%async_computation.2 | async-start | bytes 262144 | tf_op jit(solution)/shard_map/all_to_all | solution.py:98
  117.9 2.3 %convolution_convert_fusion = bf16[1024,512]{1,0:T(8,128)(2,1)} fusion(bf16[1024,1024]{1,0:T(8,128)(2,1)S(1)} %bitcast.101, bf16[512,512]{0,1:T(8,128)(2,1)S(1)} %collective-permute-done.1, bf16[256,512]{0,1:T(8,128)(2,1)S(1)} %collective-permute-done, bf16[256,512]{0,1:T(8,128)(2,1)S(1)} %bitcast.105), kind=kOutput, calls=%fused_computation | convolution fusion | flops 1077411840 | bytes 4194304 | tf_op jit(solution)/shard_map/dot_general | solution.py:77
  120.1 10.7 %all-to-all-done.2 = f32[32,1,1024]{2,1,0:T(1,128)S(1)} async-done(((f32[32,1,1024]{2,1,0:T(1,128)}), f32[32,1,1024]{2,1,0:T(1,128)S(1)}, u32[]{:S(2)}, u32[]{:S(2)}) %all-to-all-start.2) | async-done | bytes 131104 | tf_op jit(solution)/shard_map/all_to_all | solution.py:98
  130.9 3.6 %all-to-all-start.1 = ((bf16[8,128,512]{2,1,0:T(8,128)(2,1)}), bf16[8,128,512]{2,1,0:T(8,128)(2,1)S(1)}, u32[]{:S(2)}, u32[]{:S(2)}) async-start(bf16[8,128,512]{2,1,0:T(8,128)(2,1)} %bitcast.5), calls=%async_computation.1 | async-start | bytes 2097152 | tf_op jit(solution)/shard_map/all_to_all | solution.py:78
  134.5 0.6 multiply_subtract_fusion
  135.2 2.4 %collective-permute-start.3 = (bf16[256,512]{0,1:T(8,128)(2,1)S(1)}, bf16[256,512]{0,1:T(8,128)(2,1)S(1)}, u32[]{:S(2)}, u32[]{:S(2)}) collective-permute-start(bf16[256,512]{0,1:T(8,128)(2,1)S(1)} %slice.175), channel_id=1, source_target_pairs={{0,16},{16,0},{1,17},{17,1},{2,18},{18,2},{3,19},{19,3},{4,20},{20... | collective-permute-start | bytes 786440 | tf_op jit(solution)/shard_map/ppermute | solution.py:56
  137.5 0.3 reduce.2
  137.9 0.1 reshape.196
  138.2 0.7 div.9
  138.9 11.3 %collective-permute-done.3 = bf16[256,512]{0,1:T(8,128)(2,1)S(1)} collective-permute-done((bf16[256,512]{0,1:T(8,128)(2,1)S(1)}, bf16[256,512]{0,1:T(8,128)(2,1)S(1)}, u32[]{:S(2)}, u32[]{:S(2)}) %collective-permute-start.3) | collective-permute-done | bytes 262176 | tf_op jit(solution)/shard_map/ppermute | solution.py:56
  150.1 0.1 fusion.12
  150.2 0.8 copy.41
  151.1 12.4 %all-to-all-done.1 = bf16[8,128,512]{2,1,0:T(8,128)(2,1)S(1)} async-done(((bf16[8,128,512]{2,1,0:T(8,128)(2,1)}), bf16[8,128,512]{2,1,0:T(8,128)(2,1)S(1)}, u32[]{:S(2)}, u32[]{:S(2)}) %all-to-all-start.1) | async-done | bytes 1048608 | tf_op jit(solution)/shard_map/all_to_all | solution.py:78
  163.5 0.8 reduce_sum.39
  (24 shorter events, 0.4 us)
Async XLA Ops:
  7.2 1.6 copy-start
  8.8 0.8 copy-start.1
  12.7 8.5 %copy-start.4 = (bf16[1,256,512]{2,1,0:T(8,128)(2,1)S(1)}, bf16[1,256,512]{2,1,0:T(8,128)(2,1)}, u32[]{:S(2)}) copy-start(bf16[1,256,512]{2,1,0:T(8,128)(2,1)} %param.9) | copy-start | bytes 786436
  12.7 67.2 %all-to-all-start = ((bf16[8,128,1024]{2,1,0:T(8,128)(2,1)}), bf16[8,128,1024]{2,1,0:T(8,128)(2,1)S(1)}, u32[]{:S(2)}, u32[]{:S(2)}) async-start(bf16[8,128,1024]{2,1,0:T(8,128)(2,1)} %shard_map.110), calls=%async_computation | async-start | bytes 4194304 | tf_op jit(solution)/shard_map/all_to_all | solution.py:74
  20.5 59.4 %all-gather.3.cloned.1.call-start = ((), (), s32[]{:S(2)}) async-start(), calls=%async_computation.4 | async-start | bytes 1179648 | tf_op jit(solution)/shard_map/all_gather | solution.py:75
  21.4 16.3 %collective-permute-start = (bf16[256,512]{0,1:T(8,128)(2,1)S(1)}, bf16[256,512]{0,1:T(8,128)(2,1)S(1)}, u32[]{:S(2)}, u32[]{:S(2)}) collective-permute-start(bf16[256,512]{0,1:T(8,128)(2,1)S(1)} %bitcast.102), channel_id=1, source_target_pairs={{0,16},{16,0},{1,17},{17,1},{2,18},{18,2},{3,19},{19,3},{4,20},{20... | collective-permute-start | bytes 786440 | tf_op jit(solution)/shard_map/ppermute | solution.py:56
  37.7 9.9 %collective-permute-start.1 = (bf16[512,512]{0,1:T(8,128)(2,1)S(1)}, bf16[512,512]{0,1:T(8,128)(2,1)S(1)}, u32[]{:S(2)}, u32[]{:S(2)}) collective-permute-start(bf16[512,512]{0,1:T(8,128)(2,1)S(1)} %pad_maximum_fusion), channel_id=1, source_target_pairs={{0,1},{1,0},{2,3},{3,2},{4,5},{5,4},{6,7},{7,6},{8,9},{9,8},{10,11... | collective-permute-start | bytes 1572872 | tf_op jit(solution)/shard_map/ppermute | solution.py:56
  82.9 11.9 %collective-permute-start.2 = (f32[512,512]{0,1:T(8,128)}, f32[512,512]{0,1:T(8,128)}, u32[]{:S(2)}, u32[]{:S(2)}) collective-permute-start(f32[512,512]{0,1:T(8,128)} %get-tuple-element.29), channel_id=1, source_target_pairs={{0,1},{1,0},{2,3},{3,2},{4,5},{5,4},{6,7},{7,6},{8,9},{9,8},{10,11... | collective-permute-start | bytes 3145736 | tf_op jit(solution)/shard_map/ppermute | solution.py:56
  85.9 19.0 %all-to-all-start.3 = ((bf16[16,16,512]{2,1,0:T(8,128)(2,1)}), bf16[16,16,512]{2,1,0:T(8,128)(2,1)S(1)}, u32[]{:S(2)}, u32[]{:S(2)}) async-start(bf16[16,16,512]{2,1,0:T(8,128)(2,1)} %bitcast.15), calls=%async_computation.3 | async-start | bytes 524288 | tf_op jit(solution)/shard_map/all_to_all | solution.py:114
  105.6 25.2 %all-to-all-start.2 = ((f32[32,1,1024]{2,1,0:T(1,128)}), f32[32,1,1024]{2,1,0:T(1,128)S(1)}, u32[]{:S(2)}, u32[]{:S(2)}) async-start(f32[32,1,1024]{2,1,0:T(1,128)} %broadcast_in_dim.14), calls=%async_computation.2 | async-start | bytes 262144 | tf_op jit(solution)/shard_map/all_to_all | solution.py:98
  120.1 14.3 %copy-start.5 = (f32[16,512]{1,0:T(8,128)S(1)}, f32[16,512]{1,0:T(8,128)}, u32[]{:S(2)}) copy-start(f32[16,512]{1,0:T(8,128)} %param.12) | copy-start | bytes 98308
  120.1 14.3 %copy-start.6 = (f32[16,512]{1,0:T(8,128)S(1)}, f32[16,512]{1,0:T(8,128)}, u32[]{:S(2)}) copy-start(f32[16,512]{1,0:T(8,128)} %param.13) | copy-start | bytes 98308
  120.1 15.0 %copy-start.3 = (f32[512,512]{0,1:T(8,128)S(1)}, f32[512,512]{0,1:T(8,128)}, u32[]{:S(2)}) copy-start(f32[512,512]{0,1:T(8,128)} %get-tuple-element.23) | copy-start | bytes 3145732
  120.1 18.1 %copy-start.2 = (f32[1,8192]{1,0:T(1,128)S(1)}, f32[1,8192]{1,0:T(1,128)}, u32[]{:S(2)}) copy-start(f32[1,8192]{1,0:T(1,128)} %gain_ref.1) | copy-start | bytes 98308
  130.9 32.7 %all-to-all-start.1 = ((bf16[8,128,512]{2,1,0:T(8,128)(2,1)}), bf16[8,128,512]{2,1,0:T(8,128)(2,1)S(1)}, u32[]{:S(2)}, u32[]{:S(2)}) async-start(bf16[8,128,512]{2,1,0:T(8,128)(2,1)} %bitcast.5), calls=%async_computation.1 | async-start | bytes 2097152 | tf_op jit(solution)/shard_map/all_to_all | solution.py:78
  135.2 15.0 %collective-permute-start.3 = (bf16[256,512]{0,1:T(8,128)(2,1)S(1)}, bf16[256,512]{0,1:T(8,128)(2,1)S(1)}, u32[]{:S(2)}, u32[]{:S(2)}) collective-permute-start(bf16[256,512]{0,1:T(8,128)(2,1)S(1)} %slice.175), channel_id=1, source_target_pairs={{0,16},{16,0},{1,17},{17,1},{2,18},{18,2},{3,19},{19,3},{4,20},{20... | collective-permute-start | bytes 786440 | tf_op jit(solution)/shard_map/ppermute | solution.py:56
Sparse Core Ops, SparseCore 0:
  23.4 56.4 all-gather.2

commit v3 on v2

v3 whole, which is shorter than its diff:
```python
import jax
import jax.numpy as jnp
from jax import lax
from jax.experimental import pallas as pl
from jax.experimental.pallas import tpu as pltpu
from jax.sharding import Mesh, PartitionSpec as P

epsilon = 1e-05
F32 = jnp.float32
BF16 = jnp.bfloat16
FSDP = ("z", "y", "core")
VMEM_LIMIT = 48 * 1024 * 1024


def norm_kernel(place, x_ref, gain_ref, weight_ref, local_ref, weight_out, local_out, *out_refs):
    weight_out[...] = weight_ref[...]
    local_out[...] = local_ref[...]
    slots = len(out_refs)
    part = out_refs[0].shape[1] // 4
    half = x_ref.shape[1] // 2
    values = x_ref[...].astype(F32)
    total = jnp.sum(values * values, axis=1, keepdims=True)
    inverse = lax.rsqrt(total / x_ref.shape[1] + epsilon)
    for step in range(slots):
        slot = lax.rem(place[2] + step, slots)
        for piece in range(4):
            z = place[0] ^ (piece & 1)
            core = place[1] ^ (piece >> 1)
            start = pl.multiple_of(z * half + slot * 2 * part + core * part, part)
            block = x_ref[:, pl.ds(start, part)].astype(F32)
            scale = gain_ref[:, pl.ds(start, part)]
            out_refs[step][:, piece * part:(piece + 1) * part] = (
                (block * inverse) * scale
            ).astype(BF16)


def norm(place, x, gain, weight, local, slots):
    tokens, width = x.shape
    rows = 32
    steps = tokens // rows
    handed = pl.BlockSpec((weight.shape[0] // steps, weight.shape[1]), lambda i, place: (i, 0))
    return pl.pallas_call(
        norm_kernel,
        out_shape=[jax.ShapeDtypeStruct(weight.shape, BF16)] * 2
        + [jax.ShapeDtypeStruct((tokens, width // slots), BF16)] * slots,
        grid_spec=pltpu.PrefetchScalarGridSpec(
            num_scalar_prefetch=1,
            grid=(steps,),
            in_specs=[
                pl.BlockSpec((rows, width), lambda i, place: (i, 0)),
                pl.BlockSpec((1, width), lambda i, place: (0, 0)),
                handed,
                handed,
            ],
            out_specs=[handed] * 2
            + [pl.BlockSpec((rows, width // slots), lambda i, place: (i, 0))] * slots,
        ),
        compiler_params=pltpu.CompilerParams(vmem_limit_bytes=VMEM_LIMIT),
        cost_estimate=pl.CostEstimate(
            flops=6 * tokens * width, bytes_accessed=4 * tokens * width, transcendentals=tokens
        ),
    )(place, x, gain, weight, local)


def key_kernel(place, *refs):
    blocks, weights, (_, out_ref) = refs[:-6], refs[-6:-2], refs[-2:]
    slots, tokens = len(blocks), blocks[0].shape[0]
    values = jnp.concatenate([block[...] for block in blocks], axis=0)
    weight = jnp.concatenate([ref[...] for ref in weights], axis=0)
    terms = jnp.dot(values, weight, preferred_element_type=F32)
    for step in range(slots):
        source = lax.rem(place[2] + slots - step, slots)
        out_ref[source] = terms[step * tokens:(step + 1) * tokens]


def key_products(place, blocks, weights, before):
    slots, tokens = len(blocks), blocks[0].shape[0]
    part, keys = weights[0].shape
    return pl.pallas_call(
        key_kernel,
        out_shape=jax.ShapeDtypeStruct((slots, tokens, keys), F32),
        in_specs=[pl.BlockSpec(memory_space=pltpu.SMEM)]
        + [pl.BlockSpec(memory_space=pltpu.VMEM)] * (slots + 4)
        + [pl.BlockSpec(memory_space=pl.ANY)],
        out_specs=pl.BlockSpec(memory_space=pltpu.VMEM),
        compiler_params=pltpu.CompilerParams(vmem_limit_bytes=VMEM_LIMIT),
        cost_estimate=pl.CostEstimate(
            flops=8 * slots * tokens * part * keys, bytes_accessed=6 << 20, transcendentals=0
        ),
    )(place, *blocks, *weights, before)


def grad_part(place, blocks, upstream_ref, weights, first):
    slots = len(blocks)
    width = 2 * weights[0].shape[0]
    values = jnp.concatenate([block[:, first:first + width] for block in blocks], axis=0)
    upstream = jnp.concatenate(
        [upstream_ref[lax.rem(place[2] + slots - step, slots)] for step in range(slots)], axis=0
    )
    grad = lax.dot_general(
        values, upstream, (((0,), (0,)), ((), ())), preferred_element_type=F32
    )
    products = grad * jnp.concatenate([ref[...] for ref in weights], axis=0).astype(F32)
    terms = lax.dot_general(
        jnp.ones((8, products.shape[1]), F32),
        products,
        (((1,), (1,)), ((), ())),
        precision=lax.Precision.HIGHEST,
        preferred_element_type=F32,
    )
    return grad, terms


def far_kernel(place, *refs):
    blocks, (upstream_ref, *weights, _), (grad_ref, term_ref) = refs[:-6], refs[-6:-2], refs[-2:]
    grad_ref[...], term_ref[...] = grad_part(
        place, blocks, upstream_ref, weights, 2 * weights[0].shape[0]
    )


def near_kernel(place, *refs):
    blocks, (upstream_ref, *weights, other_ref), (own_ref, send_ref, term_ref) = (
        refs[:-7], refs[-7:-3], refs[-3:]
    )
    grad, term_ref[...] = grad_part(place, blocks, upstream_ref, weights, 0)
    chip = grad + other_ref[...]
    part = own_ref.shape[0]
    own_ref[...] = chip[:part]
    send_ref[...] = chip[part:].astype(BF16)


def grad_products(place, blocks, upstream, weights, before=None, other=None):
    slots, tokens = len(blocks), blocks[0].shape[0]
    part, keys = weights[0].shape
    terms = jax.ShapeDtypeStruct((8, 2 * part), F32)
    if other is None:
        shapes = (jax.ShapeDtypeStruct((2 * part, keys), F32), terms)
    else:
        shapes = (
            jax.ShapeDtypeStruct((part, keys), F32),
            jax.ShapeDtypeStruct((part, keys), BF16),
            terms,
        )
    in_vmem = pl.BlockSpec(memory_space=pltpu.VMEM)
    return pl.pallas_call(
        far_kernel if other is None else near_kernel,
        out_shape=shapes,
        in_specs=[pl.BlockSpec(memory_space=pltpu.SMEM)]
        + [in_vmem] * (slots + 3)
        + [pl.BlockSpec(memory_space=pl.ANY) if other is None else in_vmem],
        out_specs=(in_vmem,) * len(shapes),
        compiler_params=pltpu.CompilerParams(vmem_limit_bytes=VMEM_LIMIT),
        cost_estimate=pl.CostEstimate(
            flops=4 * slots * tokens * part * keys, bytes_accessed=5 << 20, transcendentals=0
        ),
    )(place, *blocks, upstream, *weights, before if other is None else other)


def swap(x, axis):
    return lax.ppermute(x, axis, [(0, 1), (1, 0)])


def body(
    activations, norm_gain, key_weight, key_cotangent, fragment_local, outer_params, outer_momentum
):
    slots = lax.axis_size("y")
    place = jnp.stack([lax.axis_index(name) for name in ("z", "core", "y")]).astype(jnp.int32)
    upstream = key_cotangent[0]
    part, keys = key_weight.shape[1:]
    tokens = upstream.shape[0]

    all_upstream = lax.all_gather(upstream, "y", axis=0, tiled=True).reshape(slots, tokens, keys)
    weight, local, *hidden = norm(
        place, activations[0], norm_gain, key_weight[0], fragment_local[0], slots
    )
    blocks = [hidden[0]] + [
        lax.ppermute(hidden[step], "y", [(i, (i + step) % slots) for i in range(slots)])
        for step in range(1, slots)
    ]
    weights = [
        weight,
        swap(weight, "z"),
        swap(weight, "core"),
        lax.ppermute(weight, ("z", "core"), [(i, 3 - i) for i in range(4)]),
    ]
    pieces = lax.all_to_all(local, "replica", 0, 0, tiled=True)

    key_terms = key_products(place, blocks, weights, pieces)
    key_out = lax.psum_scatter(
        key_terms.reshape(slots * tokens, keys), "y", scatter_dimension=0, tiled=True
    ).astype(BF16)

    far, far_terms = grad_products(place, blocks, all_upstream, weights[2:], before=key_terms)
    own, send, near_terms = grad_products(
        place, blocks, all_upstream, weights[:2], other=swap(far, "core")
    )
    grad_rows = own + swap(send, "z").astype(F32)

    terms = jnp.concatenate([near_terms[0], far_terms[0]])
    devices = 4 * slots
    spread = lax.all_to_all(
        jnp.broadcast_to(terms[None], (devices, 4 * part)), FSDP, 0, 0, tiled=True
    ).reshape(2, slots, 2, 2, 2, part)
    total = [
        [
            sum(
                spread[a, :, b, core_to ^ b, z_to ^ a]
                for a in range(2)
                for b in range(2)
            )
            for core_to in range(2)
        ]
        for z_to in range(2)
    ]
    gain_total = jnp.stack([jnp.stack(t, axis=1) for t in total]).reshape(1, -1) / norm_gain

    replicas = lax.axis_size("replica")
    own_share = jnp.sum(
        pieces.reshape(replicas, outer_params.shape[0], -1).astype(F32), axis=0
    )
    pseudo_grad = outer_params - own_share / replicas
    new_momentum = 0.9 * outer_momentum + pseudo_grad
    new_params = outer_params - 0.7 * (pseudo_grad + 0.9 * new_momentum)
    return (key_out[None], grad_rows.astype(BF16)[None], gain_total, new_params, new_momentum)


def solution(mesh):
    shape = mesh.devices.shape
    split = Mesh(
        mesh.devices.reshape(shape[0], 2, shape[1] // 4, 2), ("replica",) + FSDP
    )
    rows = P("replica", FSDP, None)
    share = P(FSDP + ("replica",), None)
    return jax.shard_map(
        body,
        mesh=split,
        in_specs=(rows, P("replica", None), rows, rows, rows, share, share),
        out_specs=(rows, rows, P("replica", None), share, share),
        check_vma=False,
    )
```

time: 172 us -> 167 us (0.971)
  waiting for transfers between devices: 81.4 us -> 29.9 us
  starting transfers between devices: 56.9 us -> 99.3 us
  matrix products: 8.55 us -> 0 us
  Pallas kernels: 3.1 us -> 10.3 us
  local copies, waits for them, and re-layouts: 4.26 us -> 7.12 us
    ppermute x0 -> x8, starting transfers between devices: none -> 43.6 us  [the longest x7 29.2 us: body(): lax.ppermute(hidden[step], 'y', [(i, (i + step) % slots) for i in range(s...]
    all_gather x1, waiting for transfers between devices: 32.2 us -> 0.02 us  [body(): lax.all_gather(upstream, 'y', axis=0, tiled=True)]
    all_to_all x3 -> x1, waiting for transfers between devices: 19.3 us -> 0.01 us  [body(): pieces = lax.all_to_all(local, 'replica', 0, 0, tiled=True)]
    all_to_all x1, starting transfers between devices: 12.3 us -> 24.8 us  [body(): lax.all_to_all(jnp.broadcast_to(terms[None], (devices, 4 * part)), FSDP,...]
    all_to_all x3 -> x1, starting transfers between devices: 20.3 us -> 9.56 us  [body(): pieces = lax.all_to_all(local, 'replica', 0, 0, tiled=True)]
    dot_general x3 -> x0, matrix products: 8.55 us -> none  [the longest x1 3.31 us: body(): lax.dot_general(columns[:, :2 * part], all_upstream, contract, preferred_...]
    pallas_call x1 -> x4, Pallas kernels: 3.1 us -> 10.3 us  [the longest x2 4.42 us: grad_products(): pl.pallas_call(far_kernel if other is None else near_kernel, out_shape=sh...]
    ppermute x0 -> x8, waiting for transfers between devices: none -> 7.17 us  [the longest x7 7.17 us: body(): lax.ppermute(hidden[step], 'y', [(i, (i + step) % slots) for i in range(s...]
  transfers between devices with their start and end apart: 9 -> 16, of which waited for: 8 -> 6; matrix products, arithmetic and copies ran while one was open for 5% -> 2% of each run, Pallas kernels for 0% -> 6%
where the time goes in v3:
time: 167 us; the launch traced here: 165 us
  starting transfers between devices  99.3 us (59%)
  waiting for transfers between devices  29.9 us (18%)
  between operations  14.3 us (9%)
  Pallas kernels  10.3 us (6%)
  local copies, waits for them, and re-layouts  7.12 us (4%)
  other arithmetic  4.26 us (3%)
    ppermute x7, starting transfers between devices, body(): lax.ppermute(hidden[step], 'y', [(i, (i + step) % slots) for i in range(s...  29.2 us
    all_to_all x1, starting transfers between devices, body(): lax.all_to_all(jnp.broadcast_to(terms[None], (devices, 4 * part)), FSDP,...  24.8 us
    ppermute x4, starting transfers between devices, swap(): return lax.ppermute(x, axis, [(0, 1), (1, 0)])  21.2 us
    ppermute x4, waiting for transfers between devices, swap(): return lax.ppermute(x, axis, [(0, 1), (1, 0)])  15.2 us
    ppermute x1, starting transfers between devices, body(): lax.ppermute(weight, ('z', 'core'), [(i, 3 - i) for i in range(4)])  14.4 us
    all_to_all x1, starting transfers between devices, body(): pieces = lax.all_to_all(local, 'replica', 0, 0, tiled=True)  9.56 us
    ppermute x7, waiting for transfers between devices, body(): lax.ppermute(hidden[step], 'y', [(i, (i + step) % slots) for i in range(s...  7.17 us
    all_to_all x1, waiting for transfers between devices, body(): lax.all_to_all(jnp.broadcast_to(terms[None], (devices, 4 * part)), FSDP,...  6.83 us
  transfers between devices with their start and end apart: 16, of which 6 were waited for; matrix products, arithmetic and copies ran while one was open for 2% of the time, Pallas kernels for 6%

profile of v3, /device:TPU:1, one launch (start us, length us, event | category | flops | bytes accessed | tf_op | source)
XLA Modules:
  0.0 165.2 jit_solution(11161870872029474132)
XLA Ops:
  8.0 1.6 copy-done.1
  9.6 0.9 copy-done.2
  10.5 0.9 copy-done.3
  11.5 0.8 copy-done.4
  12.2 2.7 %shard_map.110 = (bf16[256,512]{1,0:T(8,128)(2,1)S(1)}, bf16[256,512]{1,0:T(8,128)(2,1)}, bf16[128,1024]{1,0:T(8,128)(2,1)S(1)}, bf16[128,1024]{1,0:T(8,128)(2,1...) custom-call(s32[3]{0:T(128)S(1)} %pad_add_fusion.place, ...), custom_call_target="tpu_custom_call" | custom-call | flops 6291456 | bytes 4194304 | tf_op jit(solution)/shard_map/pallas_call | solution.py:42
  15.0 4.0 %collective-permute-start = (bf16[128,1024]{1,0:T(8,128)(2,1)S(1)}, bf16[128,1024]{1,0:T(8,128)(2,1)S(1)}, u32[]{:S(2)}, u32[]{:S(2)}) collective-permute-start(bf16[128,1024]{1,0:T(8,128)(2,1)S(1)} %get-tuple-element.21), channel_id=1, source_target_pairs={{0,2},{2,4},{4,6},{6,8},{8,10},{10,12},{12,14},{14,0},{1,3},{3,5},... | collective-permute-start | bytes 786440 | tf_op jit(solution)/shard_map/ppermute | solution.py:177
  19.0 4.2 %collective-permute-start.1 = (bf16[128,1024]{1,0:T(8,128)(2,1)S(1)}, bf16[128,1024]{1,0:T(8,128)(2,1)S(1)}, u32[]{:S(2)}, u32[]{:S(2)}) collective-permute-start(bf16[128,1024]{1,0:T(8,128)(2,1)S(1)} %get-tuple-element.22), channel_id=1, source_target_pairs={{0,4},{2,6},{4,8},{6,10},{8,12},{10,14},{12,0},{14,2},{1,5},{3,7},... | collective-permute-start | bytes 786440 | tf_op jit(solution)/shard_map/ppermute | solution.py:177
  23.2 4.6 %collective-permute-start.2 = (bf16[128,1024]{1,0:T(8,128)(2,1)S(1)}, bf16[128,1024]{1,0:T(8,128)(2,1)S(1)}, u32[]{:S(2)}, u32[]{:S(2)}) collective-permute-start(bf16[128,1024]{1,0:T(8,128)(2,1)S(1)} %get-tuple-element.23), channel_id=1, source_target_pairs={{0,6},{2,8},{4,10},{6,12},{8,14},{10,0},{12,2},{14,4},{1,7},{3,9},... | collective-permute-start | bytes 786440 | tf_op jit(solution)/shard_map/ppermute | solution.py:177
  27.9 3.5 %collective-permute-start.3 = (bf16[128,1024]{1,0:T(8,128)(2,1)S(1)}, bf16[128,1024]{1,0:T(8,128)(2,1)S(1)}, u32[]{:S(2)}, u32[]{:S(2)}) collective-permute-start(bf16[128,1024]{1,0:T(8,128)(2,1)S(1)} %get-tuple-element.24), channel_id=1, source_target_pairs={{0,8},{2,10},{4,12},{6,14},{8,0},{10,2},{12,4},{14,6},{1,9},{3,11}... | collective-permute-start | bytes 786440 | tf_op jit(solution)/shard_map/ppermute | solution.py:177
  31.4 4.9 %collective-permute-start.4 = (bf16[128,1024]{1,0:T(8,128)(2,1)S(1)}, bf16[128,1024]{1,0:T(8,128)(2,1)S(1)}, u32[]{:S(2)}, u32[]{:S(2)}) collective-permute-start(bf16[128,1024]{1,0:T(8,128)(2,1)S(1)} %get-tuple-element.25), channel_id=1, source_target_pairs={{0,10},{2,12},{4,14},{6,0},{8,2},{10,4},{12,6},{14,8},{1,11},{3,13... | collective-permute-start | bytes 786440 | tf_op jit(solution)/shard_map/ppermute | solution.py:177
  36.3 9.6 %all-to-all-start = ((bf16[16,16,512]{2,1,0:T(8,128)(2,1)}), bf16[16,16,512]{2,1,0:T(8,128)(2,1)S(1)}, u32[]{:S(2)}, u32[]{:S(2)}) async-start(bf16[16,16,512]{2,1,0:T(8,128)(2,1)} %bitcast.6), calls=%async_computation | async-start | bytes 524288 | tf_op jit(solution)/shard_map/all_to_all | solution.py:186
  45.9 5.0 %collective-permute-start.5 = (bf16[128,1024]{1,0:T(8,128)(2,1)}, bf16[128,1024]{1,0:T(8,128)(2,1)S(1)}, u32[]{:S(2)}, u32[]{:S(2)}) collective-permute-start(bf16[128,1024]{1,0:T(8,128)(2,1)} %get-tuple-element.26), channel_id=1, source_target_pairs={{0,12},{2,14},{4,0},{6,2},{8,4},{10,6},{12,8},{14,10},{1,13},{3,15... | collective-permute-start | bytes 786440 | tf_op jit(solution)/shard_map/ppermute | solution.py:177
  50.9 3.0 %collective-permute-start.6 = (bf16[128,1024]{1,0:T(8,128)(2,1)}, bf16[128,1024]{1,0:T(8,128)(2,1)S(1)}, u32[]{:S(2)}, u32[]{:S(2)}) collective-permute-start(bf16[128,1024]{1,0:T(8,128)(2,1)} %get-tuple-element.27), channel_id=1, source_target_pairs={{0,14},{2,0},{4,2},{6,4},{8,6},{10,8},{12,10},{14,12},{1,15},{3,1}... | collective-permute-start | bytes 786440 | tf_op jit(solution)/shard_map/ppermute | solution.py:177
  53.9 5.8 %collective-permute-done.2.refs_3_ = bf16[128,1024]{1,0:T(8,128)(2,1)S(1)} collective-permute-done((bf16[128,1024]{1,0:T(8,128)(2,1)S(1)}, bf16[128,1024]{1,0:T(8,128)(2,1)S(1)}, u32[]{:S(2)}, u32[]{:S(2)}) %collective-permute-start.2) | collective-permute-done | bytes 262176 | tf_op jit(solution)/shard_map/ppermute | solution.py:177
  59.7 14.4 %collective-permute-start.9 = (bf16[256,512]{1,0:T(8,128)(2,1)S(1)}, bf16[256,512]{1,0:T(8,128)(2,1)S(1)}, u32[]{:S(2)}, u32[]{:S(2)}) collective-permute-start(bf16[256,512]{1,0:T(8,128)(2,1)S(1)} %get-tuple-element.28.refs_8_.refs_9_), channel_id=1, source_target_pairs={{0,17},{1,16},{16,1},{17,0},{2,19},{3,18},{18,3},{19,2},{4,21},{5,... | collective-permute-start | bytes 786440 | tf_op jit(solution)/shard_map/ppermute | solution.py:184
  74.1 1.9 %collective-permute-start.8 = (bf16[256,512]{1,0:T(8,128)(2,1)S(1)}, bf16[256,512]{1,0:T(8,128)(2,1)S(1)}, u32[]{:S(2)}, u32[]{:S(2)}) collective-permute-start(bf16[256,512]{1,0:T(8,128)(2,1)S(1)} %get-tuple-element.28.refs_8_.refs_9_), channel_id=1, source_target_pairs={{0,1},{1,0},{2,3},{3,2},{4,5},{5,4},{6,7},{7,6},{8,9},{9,8},{10,11... | collective-permute-start | bytes 786440 | tf_op jit(solution)/shard_map/ppermute | solution.py:160
  76.1 9.6 %collective-permute-start.7 = (bf16[256,512]{1,0:T(8,128)(2,1)S(1)}, bf16[256,512]{1,0:T(8,128)(2,1)S(1)}, u32[]{:S(2)}, u32[]{:S(2)}) collective-permute-start(bf16[256,512]{1,0:T(8,128)(2,1)S(1)} %get-tuple-element.28.refs_8_.refs_9_), channel_id=1, source_target_pairs={{0,16},{16,0},{1,17},{17,1},{2,18},{18,2},{3,19},{19,3},{4,20},{20... | collective-permute-start | bytes 786440 | tf_op jit(solution)/shard_map/ppermute | solution.py:160
  85.7 1.4 collective-permute-done.6.refs_7_
  87.0 7.5 %collective-permute-done.7.refs_9_.refs_10_ = bf16[256,512]{1,0:T(8,128)(2,1)S(1)} collective-permute-done((bf16[256,512]{1,0:T(8,128)(2,1)S(1)}, bf16[256,512]{1,0:T(8,128)(2,1)S(1)}, u32[]{:S(2)}, u32[]{:S(2)}) %collective-permute-start.7) | collective-permute-done | bytes 262176 | tf_op jit(solution)/shard_map/ppermute | solution.py:160
  94.5 3.1 %shard_map.111.refs_11_ = f32[8,128,512]{2,1,0:T(8,128)} custom-call(s32[3]{0:T(128)S(1)} %pad_add_fusion.place, bf16[128,1024]{1,0:T(8,128)(2,1)S(1)} %get-tuple-element.20.refs_0_, bf16[128,1024]{1,0:T(8,128)(2,1)S(1)} %collective-permute-done.refs_1_, bf16[128,1024]{1,0:T(8,128)(2,1)S(1)} %collective-permute-done.1.refs_2_, ...), custom_call_target="tpu_custom_call" | custom-call | flops 1073741824 | bytes 6291456 | tf_op jit(solution)/shard_map/pallas_call | solution.py:79
  97.7 1.2 copy-done
  98.9 2.2 %shard_map.112 = (f32[512,512]{1,0:T(8,128)S(1)}, f32[8,512]{1,0:T(8,128)S(1)}) custom-call(s32[3]{0:T(128)S(1)} %pad_add_fusion.place, bf16[128,1024]{1,0:T(8,128)(2,1)S(1)} %get-tuple-element.20.refs_0_, bf16[128,1024]{1,0:T(8,128)(2,1)S(1)} %collective-permute-done.refs_1_, bf16[128,1024]{1,0:T(8,128)(2,1)S(1)} %collective-permute-done.1.refs_2_, ...), custom_call_target="tpu_custom_call" | custom-call | flops 536870912 | bytes 5242880 | tf_op jit(solution)/shard_map/pallas_call | solution.py:145
  101.1 2.5 %collective-permute-start.10 = (f32[512,512]{1,0:T(8,128)S(1)}, f32[512,512]{1,0:T(8,128)S(1)}, u32[]{:S(2)}, u32[]{:S(2)}) collective-permute-start(f32[512,512]{1,0:T(8,128)S(1)} %get-tuple-element.30), channel_id=1, source_target_pairs={{0,1},{1,0},{2,3},{3,2},{4,5},{5,4},{6,7},{7,6},{8,9},{9,8},{10,11... | collective-permute-start | bytes 3145736 | tf_op jit(solution)/shard_map/ppermute | solution.py:160
  103.6 2.2 %collective-permute-done.10.refs_11_ = f32[512,512]{1,0:T(8,128)S(1)} collective-permute-done((f32[512,512]{1,0:T(8,128)S(1)}, f32[512,512]{1,0:T(8,128)S(1)}, u32[]{:S(2)}, u32[]{:S(2)}) %collective-permute-start.10) | collective-permute-done | bytes 1048608 | tf_op jit(solution)/shard_map/ppermute | solution.py:160
  105.8 2.2 %shard_map.113 = (f32[256,512]{1,0:T(8,128)S(1)}, bf16[256,512]{1,0:T(8,128)(2,1)S(1)}, f32[8,512]{1,0:T(8,128)S(1)}) custom-call(s32[3]{0:T(128)S(1)} %pad_add_fusion.place, bf16[128,1024]{1,0:T(8,128)(2,1)S(1)} %get-tuple-element.20.refs_0_, bf16[128,1024]{1,0:T(8,128)(2,1)S(1)} %collective-permute-done.refs_1_, ...), custom_call_target="tpu_custom_call" | custom-call | flops 536870912 | bytes 5242880 | tf_op jit(solution)/shard_map/pallas_call | solution.py:145
  108.1 0.7 copy-done.6
  109.5 24.8 %all-to-all-start.1 = ((f32[32,1,1024]{2,1,0:T(1,128)}), f32[32,1,1024]{2,1,0:T(1,128)S(1)}, u32[]{:S(2)}, u32[]{:S(2)}) async-start(f32[32,1,1024]{2,1,0:T(1,128)} %broadcast_in_dim.14), calls=%async_computation.2 | async-start | bytes 262144 | tf_op jit(solution)/shard_map/all_to_all | solution.py:201
  135.1 7.2 %collective-permute-start.11 = (bf16[256,512]{1,0:T(8,128)(2,1)}, bf16[256,512]{1,0:T(8,128)(2,1)S(1)}, u32[]{:S(2)}, u32[]{:S(2)}) collective-permute-start(bf16[256,512]{1,0:T(8,128)(2,1)} %copy-done.6), channel_id=1, source_target_pairs={{0,16},{16,0},{1,17},{17,1},{2,18},{18,2},{3,19},{19,3},{4,20},{20... | collective-permute-start | bytes 786440 | tf_op jit(solution)/shard_map/ppermute | solution.py:160
  142.3 6.8 %all-to-all-done.1 = f32[32,1,1024]{2,1,0:T(1,128)S(1)} async-done(((f32[32,1,1024]{2,1,0:T(1,128)}), f32[32,1,1024]{2,1,0:T(1,128)S(1)}, u32[]{:S(2)}, u32[]{:S(2)}) %all-to-all-start.1) | async-done | bytes 131104 | tf_op jit(solution)/shard_map/all_to_all | solution.py:201
  150.4 5.5 %collective-permute-done.11 = bf16[256,512]{1,0:T(8,128)(2,1)S(1)} collective-permute-done((bf16[256,512]{1,0:T(8,128)(2,1)}, bf16[256,512]{1,0:T(8,128)(2,1)S(1)}, u32[]{:S(2)}, u32[]{:S(2)}) %collective-permute-start.11) | collective-permute-done | bytes 262176 | tf_op jit(solution)/shard_map/ppermute | solution.py:160
  156.0 0.8 fusion
  156.7 1.6 convert_bitcast_fusion
  (41 shorter events, 3.6 us)
Async XLA Ops:
  7.2 90.5 %all-gather.3.cloned.1.call-start = ((), (), s32[]{:S(2)}) async-start(), calls=%async_computation.4 | async-start | bytes 1179648 | tf_op jit(solution)/shard_map/all_gather | solution.py:172
  8.0 1.6 copy-start.1
  9.6 0.9 copy-start.2
  10.5 0.9 copy-start.3
  11.5 0.8 copy-start.4
  15.0 30.9 %collective-permute-start = (bf16[128,1024]{1,0:T(8,128)(2,1)S(1)}, bf16[128,1024]{1,0:T(8,128)(2,1)S(1)}, u32[]{:S(2)}, u32[]{:S(2)}) collective-permute-start(bf16[128,1024]{1,0:T(8,128)(2,1)S(1)} %get-tuple-element.21), channel_id=1, source_target_pairs={{0,2},{2,4},{4,6},{6,8},{8,10},{10,12},{12,14},{14,0},{1,3},{3,5},... | collective-permute-start | bytes 786440 | tf_op jit(solution)/shard_map/ppermute | solution.py:177
  19.0 31.9 %collective-permute-start.1 = (bf16[128,1024]{1,0:T(8,128)(2,1)S(1)}, bf16[128,1024]{1,0:T(8,128)(2,1)S(1)}, u32[]{:S(2)}, u32[]{:S(2)}) collective-permute-start(bf16[128,1024]{1,0:T(8,128)(2,1)S(1)} %get-tuple-element.22), channel_id=1, source_target_pairs={{0,4},{2,6},{4,8},{6,10},{8,12},{10,14},{12,0},{14,2},{1,5},{3,7},... | collective-permute-start | bytes 786440 | tf_op jit(solution)/shard_map/ppermute | solution.py:177
  23.2 36.5 %collective-permute-start.2 = (bf16[128,1024]{1,0:T(8,128)(2,1)S(1)}, bf16[128,1024]{1,0:T(8,128)(2,1)S(1)}, u32[]{:S(2)}, u32[]{:S(2)}) collective-permute-start(bf16[128,1024]{1,0:T(8,128)(2,1)S(1)} %get-tuple-element.23), channel_id=1, source_target_pairs={{0,6},{2,8},{4,10},{6,12},{8,14},{10,0},{12,2},{14,4},{1,7},{3,9},... | collective-permute-start | bytes 786440 | tf_op jit(solution)/shard_map/ppermute | solution.py:177
  27.9 46.2 %collective-permute-start.3 = (bf16[128,1024]{1,0:T(8,128)(2,1)S(1)}, bf16[128,1024]{1,0:T(8,128)(2,1)S(1)}, u32[]{:S(2)}, u32[]{:S(2)}) collective-permute-start(bf16[128,1024]{1,0:T(8,128)(2,1)S(1)} %get-tuple-element.24), channel_id=1, source_target_pairs={{0,8},{2,10},{4,12},{6,14},{8,0},{10,2},{12,4},{14,6},{1,9},{3,11}... | collective-permute-start | bytes 786440 | tf_op jit(solution)/shard_map/ppermute | solution.py:177
  31.4 44.6 %collective-permute-start.4 = (bf16[128,1024]{1,0:T(8,128)(2,1)S(1)}, bf16[128,1024]{1,0:T(8,128)(2,1)S(1)}, u32[]{:S(2)}, u32[]{:S(2)}) collective-permute-start(bf16[128,1024]{1,0:T(8,128)(2,1)S(1)} %get-tuple-element.25), channel_id=1, source_target_pairs={{0,10},{2,12},{4,14},{6,0},{8,2},{10,4},{12,6},{14,8},{1,11},{3,13... | collective-permute-start | bytes 786440 | tf_op jit(solution)/shard_map/ppermute | solution.py:177
  36.3 58.2 %all-to-all-start = ((bf16[16,16,512]{2,1,0:T(8,128)(2,1)}), bf16[16,16,512]{2,1,0:T(8,128)(2,1)S(1)}, u32[]{:S(2)}, u32[]{:S(2)}) async-start(bf16[16,16,512]{2,1,0:T(8,128)(2,1)} %bitcast.6), calls=%async_computation | async-start | bytes 524288 | tf_op jit(solution)/shard_map/all_to_all | solution.py:186
  45.9 110.9 %reduce-scatter.2.cloned.1.call-start = ((), (), s32[]{:S(2)}) async-start(), calls=%async_computation.3 | async-start | bytes 2359296 | tf_op jit(solution)/shard_map/reduce_scatter | solution.py:189
  45.9 39.7 %collective-permute-start.5 = (bf16[128,1024]{1,0:T(8,128)(2,1)}, bf16[128,1024]{1,0:T(8,128)(2,1)S(1)}, u32[]{:S(2)}, u32[]{:S(2)}) collective-permute-start(bf16[128,1024]{1,0:T(8,128)(2,1)} %get-tuple-element.26), channel_id=1, source_target_pairs={{0,12},{2,14},{4,0},{6,2},{8,4},{10,6},{12,8},{14,10},{1,13},{3,15... | collective-permute-start | bytes 786440 | tf_op jit(solution)/shard_map/ppermute | solution.py:177
  50.9 36.1 %collective-permute-start.6 = (bf16[128,1024]{1,0:T(8,128)(2,1)}, bf16[128,1024]{1,0:T(8,128)(2,1)S(1)}, u32[]{:S(2)}, u32[]{:S(2)}) collective-permute-start(bf16[128,1024]{1,0:T(8,128)(2,1)} %get-tuple-element.27), channel_id=1, source_target_pairs={{0,14},{2,0},{4,2},{6,4},{8,6},{10,8},{12,10},{14,12},{1,15},{3,1}... | collective-permute-start | bytes 786440 | tf_op jit(solution)/shard_map/ppermute | solution.py:177
  59.7 27.3 %collective-permute-start.9 = (bf16[256,512]{1,0:T(8,128)(2,1)S(1)}, bf16[256,512]{1,0:T(8,128)(2,1)S(1)}, u32[]{:S(2)}, u32[]{:S(2)}) collective-permute-start(bf16[256,512]{1,0:T(8,128)(2,1)S(1)} %get-tuple-element.28.refs_8_.refs_9_), channel_id=1, source_target_pairs={{0,17},{1,16},{16,1},{17,0},{2,19},{3,18},{18,3},{19,2},{4,21},{5,... | collective-permute-start | bytes 786440 | tf_op jit(solution)/shard_map/ppermute | solution.py:184
  74.1 12.9 %collective-permute-start.8 = (bf16[256,512]{1,0:T(8,128)(2,1)S(1)}, bf16[256,512]{1,0:T(8,128)(2,1)S(1)}, u32[]{:S(2)}, u32[]{:S(2)}) collective-permute-start(bf16[256,512]{1,0:T(8,128)(2,1)S(1)} %get-tuple-element.28.refs_8_.refs_9_), channel_id=1, source_target_pairs={{0,1},{1,0},{2,3},{3,2},{4,5},{5,4},{6,7},{7,6},{8,9},{9,8},{10,11... | collective-permute-start | bytes 786440 | tf_op jit(solution)/shard_map/ppermute | solution.py:160
  76.1 18.4 %collective-permute-start.7 = (bf16[256,512]{1,0:T(8,128)(2,1)S(1)}, bf16[256,512]{1,0:T(8,128)(2,1)S(1)}, u32[]{:S(2)}, u32[]{:S(2)}) collective-permute-start(bf16[256,512]{1,0:T(8,128)(2,1)S(1)} %get-tuple-element.28.refs_8_.refs_9_), channel_id=1, source_target_pairs={{0,16},{16,0},{1,17},{17,1},{2,18},{18,2},{3,19},{19,3},{4,20},{20... | collective-permute-start | bytes 786440 | tf_op jit(solution)/shard_map/ppermute | solution.py:160
  97.7 1.2 copy-start
  101.1 4.8 %collective-permute-start.10 = (f32[512,512]{1,0:T(8,128)S(1)}, f32[512,512]{1,0:T(8,128)S(1)}, u32[]{:S(2)}, u32[]{:S(2)}) collective-permute-start(f32[512,512]{1,0:T(8,128)S(1)} %get-tuple-element.30), channel_id=1, source_target_pairs={{0,1},{1,0},{2,3},{3,2},{4,5},{5,4},{6,7},{7,6},{8,9},{9,8},{10,11... | collective-permute-start | bytes 3145736 | tf_op jit(solution)/shard_map/ppermute | solution.py:160
  103.6 30.8 %copy-start.7 = (f32[16,512]{1,0:T(8,128)S(1)}, f32[16,512]{1,0:T(8,128)}, u32[]{:S(2)}) copy-start(f32[16,512]{1,0:T(8,128)} %param.12) | copy-start | bytes 98308
  103.6 30.8 %copy-start.8 = (f32[16,512]{1,0:T(8,128)S(1)}, f32[16,512]{1,0:T(8,128)}, u32[]{:S(2)}) copy-start(f32[16,512]{1,0:T(8,128)} %param.13) | copy-start | bytes 98308
  103.6 46.2 %copy-start.5 = (f32[1,8192]{1,0:T(1,128)S(1)}, f32[1,8192]{1,0:T(1,128)}, u32[]{:S(2)}) copy-start(f32[1,8192]{1,0:T(1,128)} %gain_ref.1) | copy-start | bytes 98308
  108.1 0.7 copy-start.6
  109.5 39.6 %all-to-all-start.1 = ((f32[32,1,1024]{2,1,0:T(1,128)}), f32[32,1,1024]{2,1,0:T(1,128)S(1)}, u32[]{:S(2)}, u32[]{:S(2)}) async-start(f32[32,1,1024]{2,1,0:T(1,128)} %broadcast_in_dim.14), calls=%async_computation.2 | async-start | bytes 262144 | tf_op jit(solution)/shard_map/all_to_all | solution.py:201
  135.1 20.9 %collective-permute-start.11 = (bf16[256,512]{1,0:T(8,128)(2,1)}, bf16[256,512]{1,0:T(8,128)(2,1)S(1)}, u32[]{:S(2)}, u32[]{:S(2)}) collective-permute-start(bf16[256,512]{1,0:T(8,128)(2,1)} %copy-done.6), channel_id=1, source_target_pairs={{0,16},{16,0},{1,17},{17,1},{2,18},{18,2},{3,19},{19,3},{4,20},{20... | collective-permute-start | bytes 786440 | tf_op jit(solution)/shard_map/ppermute | solution.py:160
Sparse Core Ops, SparseCore 0:
  10.1 69.2 all-gather.2
  97.8 55.8 reduce-scatter.1

commit v4 on v2

v4 whole, which is shorter than its diff:
```python
import jax
import jax.numpy as jnp
from jax import lax
from jax.experimental import pallas as pl
from jax.experimental.pallas import tpu as pltpu
from jax.sharding import Mesh, PartitionSpec as P

epsilon = 1e-05
F32 = jnp.float32
BF16 = jnp.bfloat16
REPLICA = ("x", "depth")
FSDP = ("z", "y", "core")
VMEM_LIMIT = 48 * 1024 * 1024
NORM_VMEM_LIMIT = 60 * 1024 * 1024


def norm_kernel(place, x_ref, gain_ref, out_ref):
    slots, _, width = out_ref.shape
    part = width // 4
    half = x_ref.shape[1] // 2
    values = x_ref[...].astype(F32)
    total = jnp.sum(values * values, axis=1, keepdims=True)
    inverse = lax.rsqrt(total / x_ref.shape[1] + epsilon)
    for slot in range(slots):
        for piece in range(4):
            z = place[0] ^ (piece & 1)
            core = place[1] ^ (piece >> 1)
            start = pl.multiple_of(z * half + slot * 2 * part + core * part, part)
            block = x_ref[:, pl.ds(start, part)].astype(F32)
            scale = gain_ref[:, pl.ds(start, part)]
            out_ref[slot, :, piece * part:(piece + 1) * part] = (
                (block * inverse) * scale
            ).astype(out_ref.dtype)


def norm(place, x, gain, slots):
    tokens, width = x.shape
    rows = 32
    return pl.pallas_call(
        norm_kernel,
        out_shape=jax.ShapeDtypeStruct((slots, tokens, width // slots), BF16),
        grid_spec=pltpu.PrefetchScalarGridSpec(
            num_scalar_prefetch=1,
            grid=(tokens // rows,),
            in_specs=[
                pl.BlockSpec((rows, width), lambda i, place: (i, 0)),
                pl.BlockSpec((1, width), lambda i, place: (0, 0)),
            ],
            out_specs=pl.BlockSpec((slots, rows, width // slots), lambda i, place: (0, i, 0)),
        ),
        compiler_params=pltpu.CompilerParams(vmem_limit_bytes=NORM_VMEM_LIMIT),
        cost_estimate=pl.CostEstimate(
            flops=6 * tokens * width, bytes_accessed=4 * tokens * width, transcendentals=tokens
        ),
    )(place, x, gain)


def key_kernel(columns_ref, near_ref, far_ref, _, out_ref):
    slots, tokens, width = columns_ref.shape
    weight = jnp.concatenate([near_ref[...], far_ref[...]], axis=0)
    terms = jnp.dot(
        columns_ref[...].reshape(slots * tokens, width), weight, preferred_element_type=F32
    )
    out_ref[...] = terms.astype(out_ref.dtype)


def key_products(columns, weights, before, dtype):
    slots, tokens, width = columns.shape
    keys = weights[0].shape[1]
    in_vmem = pl.BlockSpec(memory_space=pltpu.VMEM)
    return pl.pallas_call(
        key_kernel,
        out_shape=jax.ShapeDtypeStruct((slots * tokens, keys), dtype),
        in_specs=[in_vmem] * 3 + [pl.BlockSpec(memory_space=pl.ANY)],
        out_specs=in_vmem,
        compiler_params=pltpu.CompilerParams(vmem_limit_bytes=VMEM_LIMIT),
        cost_estimate=pl.CostEstimate(
            flops=2 * slots * tokens * width * keys, bytes_accessed=5 << 20, transcendentals=0
        ),
    )(columns, *weights, before)


def grad_kernel(columns_ref, upstream_ref, _, near_ref, far_ref):
    slots, tokens, width = columns_ref.shape
    half = width // 2
    upstream = upstream_ref[...]
    for index, out_ref in ((1, far_ref), (0, near_ref)):
        values = columns_ref[:, :, index * half:(index + 1) * half]
        out_ref[...] = lax.dot_general(
            values.reshape(slots * tokens, half),
            upstream,
            (((0,), (0,)), ((), ())),
            preferred_element_type=F32,
        )


def grad_products(columns, upstream, before):
    slots, tokens, width = columns.shape
    keys = upstream.shape[1]
    in_vmem = pl.BlockSpec(memory_space=pltpu.VMEM)
    return pl.pallas_call(
        grad_kernel,
        out_shape=[jax.ShapeDtypeStruct((width // 2, keys), F32)] * 2,
        in_specs=[in_vmem] * 2 + [pl.BlockSpec(memory_space=pl.ANY)],
        out_specs=[in_vmem] * 2,
        compiler_params=pltpu.CompilerParams(vmem_limit_bytes=VMEM_LIMIT),
        cost_estimate=pl.CostEstimate(
            flops=2 * slots * tokens * width * keys, bytes_accessed=6 << 20, transcendentals=0
        ),
    )(columns, upstream, before)


def term_kernel(near_ref, far_ref, near_weight_ref, far_weight_ref, out_ref):
    half = near_ref.shape[0]
    for index, (grad_ref, weight_ref) in enumerate(
        ((near_ref, near_weight_ref), (far_ref, far_weight_ref))
    ):
        products = grad_ref[...] * weight_ref[...].astype(F32)
        out_ref[:, index * half:(index + 1) * half] = lax.dot_general(
            jnp.ones((8, products.shape[1]), F32),
            products,
            (((1,), (1,)), ((), ())),
            precision=lax.Precision.HIGHEST,
            preferred_element_type=F32,
        )


def term_rows(near, far, weights):
    in_vmem = pl.BlockSpec(memory_space=pltpu.VMEM)
    return pl.pallas_call(
        term_kernel,
        out_shape=jax.ShapeDtypeStruct((8, 2 * near.shape[0]), F32),
        in_specs=[in_vmem] * 4,
        out_specs=in_vmem,
        compiler_params=pltpu.CompilerParams(vmem_limit_bytes=32 * 1024 * 1024),
        cost_estimate=pl.CostEstimate(
            flops=16 * near.size, bytes_accessed=4 << 20, transcendentals=0
        ),
    )(near, far, *weights)


def chip_kernel(near_ref, other_ref, terms_ref, own_ref, send_ref, terms_out):
    part = own_ref.shape[0]
    own_ref[...] = near_ref[:part] + other_ref[:part]
    send_ref[...] = (near_ref[part:] + other_ref[part:]).astype(BF16)
    terms_out[...] = terms_ref[...]


def chip_sums(near, other, terms):
    part, keys = near.shape[0] // 2, near.shape[1]
    return pl.pallas_call(
        chip_kernel,
        out_shape=(
            jax.ShapeDtypeStruct((part, keys), F32),
            jax.ShapeDtypeStruct((part, keys), BF16),
            jax.ShapeDtypeStruct(terms.shape, F32),
        ),
        compiler_params=pltpu.CompilerParams(vmem_limit_bytes=16 * 1024 * 1024),
        cost_estimate=pl.CostEstimate(
            flops=near.size, bytes_accessed=10 * near.size, transcendentals=0
        ),
    )(near, other, terms)


def swap(x, axis):
    return lax.ppermute(x, axis, [(0, 1), (1, 0)])


def halved(rows, axis, bit):
    half = rows.shape[0] // 2
    upper = (lax.axis_index(axis) & bit) != 0
    sent = jnp.where(upper, rows[:half], rows[half:])
    kept = jnp.where(upper, rows[half:], rows[:half])
    size = lax.axis_size(axis)
    received = lax.ppermute(sent, axis, [(i, i ^ bit) for i in range(size)])
    return kept.astype(F32) + received.astype(F32)


def body(
    activations, norm_gain, key_weight, key_cotangent, fragment_local, outer_params, outer_momentum
):
    slots = lax.axis_size("y")
    z, core = lax.axis_index("z"), lax.axis_index("core")
    place = jnp.stack([z, core]).astype(jnp.int32)
    weight = key_weight[0]
    upstream = key_cotangent[0]
    part, keys = weight.shape
    tokens = upstream.shape[0]

    all_upstream = lax.all_gather(upstream, "y", axis=0, tiled=True)
    hidden = norm(place, activations[0], norm_gain, slots)
    columns = lax.all_to_all(hidden, "y", 0, 0, tiled=True)

    near_weight = jnp.concatenate([weight, swap(weight, "z")], axis=0)
    weights = [near_weight, swap(near_weight, "core")]

    own_share = fragment_local[0]
    for axis in REPLICA:
        for bit in (2, 1):
            own_share = halved(own_share, axis, bit)
    pseudo_grad = outer_params - own_share / (lax.axis_size("x") * lax.axis_size("depth"))
    new_momentum = 0.9 * outer_momentum + pseudo_grad
    new_params = outer_params - 0.7 * (pseudo_grad + 0.9 * new_momentum)

    key_terms = key_products(columns, weights, new_params, BF16)
    key_out = lax.psum_scatter(key_terms, "y", scatter_dimension=0, tiled=True).astype(BF16)

    near, far = grad_products(columns, all_upstream, key_terms)
    terms = term_rows(near, far, weights)
    own, send, terms = chip_sums(near, swap(far, "core"), terms)
    grad_rows = own + swap(send, "z").astype(F32)

    devices = 4 * slots
    spread = lax.all_to_all(
        jnp.broadcast_to(terms[:1], (devices, 4 * part)), FSDP, 0, 0, tiled=True
    ).reshape(2, slots, 2, 2, 2, part)
    total = [
        [
            sum(
                spread[a, :, b, core_to ^ b, z_to ^ a]
                for a in range(2)
                for b in range(2)
            )
            for core_to in range(2)
        ]
        for z_to in range(2)
    ]
    gain_total = jnp.stack([jnp.stack(t, axis=1) for t in total]).reshape(1, -1) / norm_gain
    return (key_out[None], grad_rows.astype(BF16)[None], gain_total, new_params, new_momentum)


def solution(mesh):
    replicas, devices = mesh.devices.shape
    split = Mesh(
        mesh.devices.reshape(replicas // 4, 4, 2, devices // 4, 2), REPLICA + FSDP
    )
    rows = P(REPLICA, FSDP, None)
    share = P(FSDP + REPLICA, None)
    return jax.shard_map(
        body,
        mesh=split,
        in_specs=(rows, P(REPLICA, None), rows, rows, rows, share, share),
        out_specs=(rows, rows, P(REPLICA, None), share, share),
        check_vma=False,
    )
```

time: 172 us -> 139 us (0.81)
  the two profiles are of different devices: /device:TPU:1 before, /device:TPU:2 now
where the time goes in v4:
time: 139 us; the launch traced here: 138 us
  starting transfers between devices  56.3 us (41%)
  waiting for transfers between devices  49 us (35%)
  between operations  14.3 us (10%)
  Pallas kernels  13.2 us (9%)
  other arithmetic  3.27 us (2%)
  local copies, waits for them, and re-layouts  2.14 us (2%)
    ppermute x4, starting transfers between devices, swap(): return lax.ppermute(x, axis, [(0, 1), (1, 0)])  20.5 us
    all_to_all x1, waiting for transfers between devices, body(): columns = lax.all_to_all(hidden, 'y', 0, 0, tiled=True)  15 us
    ppermute x4, starting transfers between devices, halved(): received = lax.ppermute(sent, axis, [(i, i ^ bit) for i in range(size)])  14.6 us
    all_to_all x1, starting transfers between devices, body(): lax.all_to_all(jnp.broadcast_to(terms[:1], (devices, 4 * part)), FSDP, 0,...  14 us
    ppermute x4, waiting for transfers between devices, halved(): received = lax.ppermute(sent, axis, [(i, i ^ bit) for i in range(size)])  10.2 us
    reduce_scatter x1, waiting for transfers between devices, body(): lax.psum_scatter(key_terms, 'y', scatter_dimension=0, tiled=True)  8.45 us
    all_to_all x1, waiting for transfers between devices, body(): lax.all_to_all(jnp.broadcast_to(terms[:1], (devices, 4 * part)), FSDP, 0,...  7.81 us
    ppermute x4, waiting for transfers between devices, swap(): return lax.ppermute(x, axis, [(0, 1), (1, 0)])  7.31 us
  transfers between devices with their start and end apart: 12, of which 10 were waited for; matrix products, arithmetic and copies ran while one was open for 3% of the time, Pallas kernels for 4%

profile of v4, /device:TPU:2, one launch (start us, length us, event | category | flops | bytes accessed | tf_op | source)
XLA Modules:
  0.0 138.3 jit_solution(13962357955089379073)
XLA Ops:
  7.2 0.6 pad_add_fusion.place
  7.8 5.0 %shard_map.110 = bf16[8,128,1024]{2,1,0:T(8,128)(2,1)} custom-call(s32[2]{0:T(128)} %pad_add_fusion.place, bf16[128,8192]{1,0:T(8,128)(2,1)} %bitcast.93, f32[1,8192]{1,0:T(1,128)} %gain_ref.1), custom_call_target="tpu_custom_call" | custom-call | flops 6291456 | bytes 4194304 | tf_op jit(solution)/shard_map/pallas_call | solution.py:39
  12.8 7.2 %all-to-all-start = ((bf16[8,128,1024]{2,1,0:T(8,128)(2,1)}), bf16[8,128,1024]{2,1,0:T(8,128)(2,1)S(1)}, u32[]{:S(2)}, u32[]{:S(2)}) async-start(bf16[8,128,1024]{2,1,0:T(8,128)(2,1)} %shard_map.110), calls=%async_computation | async-start | bytes 4194304 | tf_op jit(solution)/shard_map/all_to_all | solution.py:192
  20.1 4.0 %collective-permute-start.2 = (bf16[128,512]{1,0:T(8,128)(2,1)S(1)}, bf16[128,512]{1,0:T(8,128)(2,1)S(1)}, u32[]{:S(2)}, u32[]{:S(2)}) collective-permute-start(bf16[128,512]{1,0:T(8,128)(2,1)S(1)} %select_bitcast_fusion), channel_id=1, source_target_pairs={{0,256},{128,384},{256,0},{384,128},{1,257},{129,385},{257,1},{385... | collective-permute-start | bytes 393224 | tf_op jit(solution)/shard_map/ppermute | solution.py:175
  24.2 4.3 %collective-permute-done.2 = bf16[128,512]{1,0:T(8,128)(2,1)S(1)} collective-permute-done((bf16[128,512]{1,0:T(8,128)(2,1)S(1)}, bf16[128,512]{1,0:T(8,128)(2,1)S(1)}, u32[]{:S(2)}, u32[]{:S(2)}) %collective-permute-start.2) | collective-permute-done | bytes 131104 | tf_op jit(solution)/shard_map/ppermute | solution.py:175
  28.6 4.3 %collective-permute-start.3 = (f32[64,512]{1,0:T(8,128)S(1)}, f32[64,512]{1,0:T(8,128)S(1)}, u32[]{:S(2)}, u32[]{:S(2)}) collective-permute-start(f32[64,512]{1,0:T(8,128)S(1)} %slice_select_fusion), channel_id=1, source_target_pairs={{0,128},{128,0},{256,384},{384,256},{1,129},{129,1},{257,385},{385... | collective-permute-start | bytes 393224 | tf_op jit(solution)/shard_map/ppermute | solution.py:175
  32.9 9.0 %collective-permute-start = (bf16[256,512]{1,0:T(8,128)(2,1)S(1)}, bf16[256,512]{1,0:T(8,128)(2,1)S(1)}, u32[]{:S(2)}, u32[]{:S(2)}) collective-permute-start(bf16[256,512]{1,0:T(8,128)(2,1)S(1)} %bitcast.94), channel_id=1, source_target_pairs={{0,16},{16,0},{1,17},{17,1},{2,18},{18,2},{3,19},{19,3},{4,20},{20... | collective-permute-start | bytes 786440 | tf_op jit(solution)/shard_map/ppermute | solution.py:166
  42.0 4.3 %collective-permute-start.4 = (f32[32,512]{1,0:T(8,128)S(1)}, f32[32,512]{1,0:T(8,128)S(1)}, u32[]{:S(2)}, u32[]{:S(2)}) collective-permute-start(f32[32,512]{1,0:T(8,128)S(1)} %slice_select_fusion.1), channel_id=1, source_target_pairs={{0,64},{32,96},{64,0},{96,32},{1,65},{33,97},{65,1},{97,33},{2,66}... | collective-permute-start | bytes 196616 | tf_op jit(solution)/shard_map/ppermute | solution.py:175
  46.3 5.8 %collective-permute-done = bf16[256,512]{1,0:T(8,128)(2,1)S(1)} collective-permute-done((bf16[256,512]{1,0:T(8,128)(2,1)S(1)}, bf16[256,512]{1,0:T(8,128)(2,1)S(1)}, u32[]{:S(2)}, u32[]{:S(2)}) %collective-permute-start) | collective-permute-done | bytes 262176 | tf_op jit(solution)/shard_map/ppermute | solution.py:166
  52.1 1.9 %collective-permute-start.1 = (bf16[512,512]{1,0:T(8,128)(2,1)S(1)}, bf16[512,512]{1,0:T(8,128)(2,1)S(1)}, u32[]{:S(2)}, u32[]{:S(2)}) collective-permute-start(bf16[512,512]{1,0:T(8,128)(2,1)S(1)} %pad_maximum_fusion.near_ref.near_weight_ref), channel_id=1, source_target_pairs={{0,1},{1,0},{2,3},{3,2},{4,5},{5,4},{6,7},{7,6},{8,9},{9,8},{10,11... | collective-permute-start | bytes 1572872 | tf_op jit(solution)/shard_map/ppermute | solution.py:166
  54.0 2.1 %collective-permute-done.4 = f32[32,512]{1,0:T(8,128)S(1)} collective-permute-done((f32[32,512]{1,0:T(8,128)S(1)}, f32[32,512]{1,0:T(8,128)S(1)}, u32[]{:S(2)}, u32[]{:S(2)}) %collective-permute-start.4) | collective-permute-done | bytes 65568 | tf_op jit(solution)/shard_map/ppermute | solution.py:175
  56.1 1.9 %collective-permute-start.5 = (f32[16,512]{1,0:T(8,128)S(1)}, f32[16,512]{1,0:T(8,128)S(1)}, u32[]{:S(2)}, u32[]{:S(2)}) collective-permute-start(f32[16,512]{1,0:T(8,128)S(1)} %slice_select_fusion.2), channel_id=1, source_target_pairs={{0,32},{32,0},{64,96},{96,64},{1,33},{33,1},{65,97},{97,65},{2,34}... | collective-permute-start | bytes 98312 | tf_op jit(solution)/shard_map/ppermute | solution.py:175
  58.1 3.9 %collective-permute-done.5 = f32[16,512]{1,0:T(8,128)S(1)} collective-permute-done((f32[16,512]{1,0:T(8,128)S(1)}, f32[16,512]{1,0:T(8,128)S(1)}, u32[]{:S(2)}, u32[]{:S(2)}) %collective-permute-start.5) | collective-permute-done | bytes 32800 | tf_op jit(solution)/shard_map/ppermute | solution.py:175
  62.0 0.6 multiply_subtract_fusion
  62.6 15.0 %all-to-all-done.columns_ref = bf16[8,128,1024]{2,1,0:T(8,128)(2,1)S(1)} async-done(((bf16[8,128,1024]{2,1,0:T(8,128)(2,1)}), bf16[8,128,1024]{2,1,0:T(8,128)(2,1)S(1)}, u32[]{:S(2)}, u32[]{:S(2)}) %all-to-all-start) | async-done | bytes 2097184 | tf_op jit(solution)/shard_map/all_to_all | solution.py:192
  77.6 2.2 %shard_map.111._ = bf16[1024,512]{1,0:T(8,128)(2,1)} custom-call(bf16[8,128,1024]{2,1,0:T(8,128)(2,1)S(1)} %all-to-all-done.columns_ref, bf16[512,512]{1,0:T(8,128)(2,1)S(1)} %pad_maximum_fusion.near_ref.near_weight_ref, bf16[512,512]{1,0:T(8,128)(2,1)S(1)} %collective-permute-done.1.far_ref.far_weight_ref, f32[16,512]{1,0:T(8,128)S(1)} %get-tuple-element.15._), custom_call_target="tpu_custom_call" | custom-call | flops 1073741824 | bytes 5242880 | tf_op jit(solution)/shard_map/pallas_call | solution.py:71
  79.8 0.2 all-gather.3.cloned.1.call-done
  80.1 1.2 copy-done.1
  81.3 2.9 %shard_map.112 = (f32[512,512]{1,0:T(8,128)S(1)}, f32[512,512]{1,0:T(8,128)S(1)}) custom-call(bf16[8,128,1024]{2,1,0:T(8,128)(2,1)} %copy-done, bf16[1024,512]{1,0:T(8,128)(2,1)S(1)} %bitcast.92, bf16[1024,512]{1,0:T(8,128)(2,1)} %shard_map.111._), custom_call_target="tpu_custom_call" | custom-call | flops 1073741824 | bytes 6291456 | tf_op jit(solution)/shard_map/pallas_call | solution.py:101
  84.2 1.9 %collective-permute-start.6 = (f32[512,512]{1,0:T(8,128)S(1)}, f32[512,512]{1,0:T(8,128)}, u32[]{:S(2)}, u32[]{:S(2)}) collective-permute-start(f32[512,512]{1,0:T(8,128)S(1)} %get-tuple-element.11.far_ref), channel_id=1, source_target_pairs={{0,1},{1,0},{2,3},{3,2},{4,5},{5,4},{6,7},{7,6},{8,9},{9,8},{10,11... | collective-permute-start | bytes 3145736 | tf_op jit(solution)/shard_map/ppermute | solution.py:166
  86.1 1.7 %shard_map.113.terms_ref = f32[8,1024]{1,0:T(8,128)S(1)} custom-call(f32[512,512]{1,0:T(8,128)S(1)} %get-tuple-element.10.near_ref, f32[512,512]{1,0:T(8,128)S(1)} %get-tuple-element.11.far_ref, bf16[512,512]{1,0:T(8,128)(2,1)S(1)} %pad_maximum_fusion.near_ref.near_weight_ref, bf16[512,512]{1,0:T(8,128)(2,1)S(1)} %collective-permute-done.1.far_ref.far_weight_ref), custom_call_target="tpu_custom_call" | custom-call | flops 4194304 | bytes 4194304 | tf_op jit(solution)/shard_map/pallas_call | solution.py:130
  87.9 1.0 collective-permute-done.6.other_ref
  88.9 1.3 shard_map.114
  90.2 0.7 broadcast_in_dim.13
  90.9 14.0 %all-to-all-start.1 = ((f32[32,1,1024]{2,1,0:T(1,128)}), f32[32,1,1024]{2,1,0:T(1,128)S(1)}, u32[]{:S(2)}, u32[]{:S(2)}) async-start(f32[32,1,1024]{2,1,0:T(1,128)} %broadcast_in_dim.13), calls=%async_computation.2 | async-start | bytes 262144 | tf_op jit(solution)/shard_map/all_to_all | solution.py:214
  104.9 7.6 %collective-permute-start.7 = (bf16[256,512]{1,0:T(8,128)(2,1)S(1)}, bf16[256,512]{1,0:T(8,128)(2,1)S(1)}, u32[]{:S(2)}, u32[]{:S(2)}) collective-permute-start(bf16[256,512]{1,0:T(8,128)(2,1)S(1)} %get-tuple-element.13), channel_id=1, source_target_pairs={{0,16},{16,0},{1,17},{17,1},{2,18},{18,2},{3,19},{19,3},{4,20},{20... | collective-permute-start | bytes 786440 | tf_op jit(solution)/shard_map/ppermute | solution.py:166
  112.5 7.8 %all-to-all-done.1 = f32[32,1,1024]{2,1,0:T(1,128)S(1)} async-done(((f32[32,1,1024]{2,1,0:T(1,128)}), f32[32,1,1024]{2,1,0:T(1,128)S(1)}, u32[]{:S(2)}, u32[]{:S(2)}) %all-to-all-start.1) | async-done | bytes 131104 | tf_op jit(solution)/shard_map/all_to_all | solution.py:214
  120.3 0.3 reduce
  121.0 0.7 div.11
  121.7 0.6 collective-permute-done.7
  122.2 0.8 fusion
  123.0 8.5 %reduce-scatter.2.cloned.1.call-done = bf16[128,512]{1,0:T(8,128)(2,1)} async-done(((bf16[1024,512]{1,0:T(8,128)(2,1)}), bf16[128,512]{1,0:T(8,128)(2,1)}) %reduce-scatter.2.cloned.1.call-update) | async-done | bytes 131088 | tf_op jit(solution)/shard_map/reduce_scatter | solution.py:206
  (36 shorter events, 0.6 us)
Async XLA Ops:
  12.8 7.3 %copy-start.3 = (bf16[1,256,512]{2,1,0:T(8,128)(2,1)S(1)}, bf16[1,256,512]{2,1,0:T(8,128)(2,1)}, u32[]{:S(2)}) copy-start(bf16[1,256,512]{2,1,0:T(8,128)(2,1)} %param.11) | copy-start | bytes 786436
  12.8 20.1 %copy-start.4 = (bf16[1,256,512]{2,1,0:T(8,128)(2,1)S(1)}, bf16[1,256,512]{2,1,0:T(8,128)(2,1)}, u32[]{:S(2)}) copy-start(bf16[1,256,512]{2,1,0:T(8,128)(2,1)} %param.9) | copy-start | bytes 786436
  12.8 64.8 %all-to-all-start = ((bf16[8,128,1024]{2,1,0:T(8,128)(2,1)}), bf16[8,128,1024]{2,1,0:T(8,128)(2,1)S(1)}, u32[]{:S(2)}, u32[]{:S(2)}) async-start(bf16[8,128,1024]{2,1,0:T(8,128)(2,1)} %shard_map.110), calls=%async_computation | async-start | bytes 4194304 | tf_op jit(solution)/shard_map/all_to_all | solution.py:192
  20.0 42.0 %copy-start.6 = (f32[16,512]{1,0:T(8,128)S(1)}, f32[16,512]{1,0:T(8,128)}, u32[]{:S(2)}) copy-start(f32[16,512]{1,0:T(8,128)} %param.12) | copy-start | bytes 98308
  20.0 42.0 %copy-start.7 = (f32[16,512]{1,0:T(8,128)S(1)}, f32[16,512]{1,0:T(8,128)}, u32[]{:S(2)}) copy-start(f32[16,512]{1,0:T(8,128)} %param.13) | copy-start | bytes 98308
  20.0 60.0 %all-gather.3.cloned.1.call-start = ((), (), s32[]{:S(2)}) async-start(), calls=%async_computation.4 | async-start | bytes 1179648 | tf_op jit(solution)/shard_map/all_gather | solution.py:190
  20.1 8.4 %collective-permute-start.2 = (bf16[128,512]{1,0:T(8,128)(2,1)S(1)}, bf16[128,512]{1,0:T(8,128)(2,1)S(1)}, u32[]{:S(2)}, u32[]{:S(2)}) collective-permute-start(bf16[128,512]{1,0:T(8,128)(2,1)S(1)} %select_bitcast_fusion), channel_id=1, source_target_pairs={{0,256},{128,384},{256,0},{384,128},{1,257},{129,385},{257,1},{385... | collective-permute-start | bytes 393224 | tf_op jit(solution)/shard_map/ppermute | solution.py:175
  24.2 107.3 %reduce-scatter.2.cloned.1.call-start = ((), (), s32[]{:S(2)}) async-start(), calls=%async_computation.3 | async-start | bytes 1179648 | tf_op jit(solution)/shard_map/reduce_scatter | solution.py:206
  28.6 13.4 %collective-permute-start.3 = (f32[64,512]{1,0:T(8,128)S(1)}, f32[64,512]{1,0:T(8,128)S(1)}, u32[]{:S(2)}, u32[]{:S(2)}) collective-permute-start(f32[64,512]{1,0:T(8,128)S(1)} %slice_select_fusion), channel_id=1, source_target_pairs={{0,128},{128,0},{256,384},{384,256},{1,129},{129,1},{257,385},{385... | collective-permute-start | bytes 393224 | tf_op jit(solution)/shard_map/ppermute | solution.py:175
  32.9 19.2 %collective-permute-start = (bf16[256,512]{1,0:T(8,128)(2,1)S(1)}, bf16[256,512]{1,0:T(8,128)(2,1)S(1)}, u32[]{:S(2)}, u32[]{:S(2)}) collective-permute-start(bf16[256,512]{1,0:T(8,128)(2,1)S(1)} %bitcast.94), channel_id=1, source_target_pairs={{0,16},{16,0},{1,17},{17,1},{2,18},{18,2},{3,19},{19,3},{4,20},{20... | collective-permute-start | bytes 786440 | tf_op jit(solution)/shard_map/ppermute | solution.py:166
  42.0 14.1 %collective-permute-start.4 = (f32[32,512]{1,0:T(8,128)S(1)}, f32[32,512]{1,0:T(8,128)S(1)}, u32[]{:S(2)}, u32[]{:S(2)}) collective-permute-start(f32[32,512]{1,0:T(8,128)S(1)} %slice_select_fusion.1), channel_id=1, source_target_pairs={{0,64},{32,96},{64,0},{96,32},{1,65},{33,97},{65,1},{97,33},{2,66}... | collective-permute-start | bytes 196616 | tf_op jit(solution)/shard_map/ppermute | solution.py:175
  52.1 10.5 %collective-permute-start.1 = (bf16[512,512]{1,0:T(8,128)(2,1)S(1)}, bf16[512,512]{1,0:T(8,128)(2,1)S(1)}, u32[]{:S(2)}, u32[]{:S(2)}) collective-permute-start(bf16[512,512]{1,0:T(8,128)(2,1)S(1)} %pad_maximum_fusion.near_ref.near_weight_ref), channel_id=1, source_target_pairs={{0,1},{1,0},{2,3},{3,2},{4,5},{5,4},{6,7},{7,6},{8,9},{9,8},{10,11... | collective-permute-start | bytes 1572872 | tf_op jit(solution)/shard_map/ppermute | solution.py:166
  56.1 5.8 %collective-permute-start.5 = (f32[16,512]{1,0:T(8,128)S(1)}, f32[16,512]{1,0:T(8,128)S(1)}, u32[]{:S(2)}, u32[]{:S(2)}) collective-permute-start(f32[16,512]{1,0:T(8,128)S(1)} %slice_select_fusion.2), channel_id=1, source_target_pairs={{0,32},{32,0},{64,96},{96,64},{1,33},{33,1},{65,97},{97,65},{2,34}... | collective-permute-start | bytes 98312 | tf_op jit(solution)/shard_map/ppermute | solution.py:175
  62.6 17.2 %copy-start.2 = (f32[16,512]{1,0:T(8,128)}, f32[16,512]{1,0:T(8,128)S(1)}, u32[]{:S(2)}) copy-start(f32[16,512]{1,0:T(8,128)S(1)} %get-tuple-element.15._) | copy-start | bytes 98308
  77.6 2.3 %copy-start = (bf16[8,128,1024]{2,1,0:T(8,128)(2,1)}, bf16[8,128,1024]{2,1,0:T(8,128)(2,1)S(1)}, u32[]{:S(2)}) copy-start(bf16[8,128,1024]{2,1,0:T(8,128)(2,1)S(1)} %all-to-all-done.columns_ref) | copy-start | bytes 6291460
  80.1 1.2 copy-start.1
  84.2 4.7 %collective-permute-start.6 = (f32[512,512]{1,0:T(8,128)S(1)}, f32[512,512]{1,0:T(8,128)}, u32[]{:S(2)}, u32[]{:S(2)}) collective-permute-start(f32[512,512]{1,0:T(8,128)S(1)} %get-tuple-element.11.far_ref), channel_id=1, source_target_pairs={{0,1},{1,0},{2,3},{3,2},{4,5},{5,4},{6,7},{7,6},{8,9},{9,8},{10,11... | collective-permute-start | bytes 3145736 | tf_op jit(solution)/shard_map/ppermute | solution.py:166
  87.9 33.1 %copy-start.5 = (f32[1,8192]{1,0:T(1,128)S(1)}, f32[1,8192]{1,0:T(1,128)}, u32[]{:S(2)}) copy-start(f32[1,8192]{1,0:T(1,128)} %gain_ref.1) | copy-start | bytes 98308
  90.9 29.4 %all-to-all-start.1 = ((f32[32,1,1024]{2,1,0:T(1,128)}), f32[32,1,1024]{2,1,0:T(1,128)S(1)}, u32[]{:S(2)}, u32[]{:S(2)}) async-start(f32[32,1,1024]{2,1,0:T(1,128)} %broadcast_in_dim.13), calls=%async_computation.2 | async-start | bytes 262144 | tf_op jit(solution)/shard_map/all_to_all | solution.py:214
  104.9 17.3 %collective-permute-start.7 = (bf16[256,512]{1,0:T(8,128)(2,1)S(1)}, bf16[256,512]{1,0:T(8,128)(2,1)S(1)}, u32[]{:S(2)}, u32[]{:S(2)}) collective-permute-start(bf16[256,512]{1,0:T(8,128)(2,1)S(1)} %get-tuple-element.13), channel_id=1, source_target_pairs={{0,16},{16,0},{1,17},{17,1},{2,18},{18,2},{3,19},{19,3},{4,20},{20... | collective-permute-start | bytes 786440 | tf_op jit(solution)/shard_map/ppermute | solution.py:166
Sparse Core Ops, SparseCore 0:
  24.3 55.7 all-gather.2
  86.2 45.1 reduce-scatter.1

commit v5 on v4

--- a/solution.py
+++ b/solution.py
@@ -14,7 +14,7 @@
 NORM_VMEM_LIMIT = 60 * 1024 * 1024
 
 
-def norm_kernel(place, x_ref, gain_ref, out_ref):
+def norm_kernel(x_ref, gain_ref, out_ref):
     slots, _, width = out_ref.shape
     part = width // 4
     half = x_ref.shape[1] // 2
@@ -23,8 +23,8 @@
     inverse = lax.rsqrt(total / x_ref.shape[1] + epsilon)
     for slot in range(slots):
         for piece in range(4):
-            z = place[0] ^ (piece & 1)
-            core = place[1] ^ (piece >> 1)
+            z = lax.axis_index("z") ^ (piece & 1)
+            core = lax.axis_index("core") ^ (piece >> 1)
             start = pl.multiple_of(z * half + slot * 2 * part + core * part, part)
             block = x_ref[:, pl.ds(start, part)].astype(F32)
             scale = gain_ref[:, pl.ds(start, part)]
@@ -33,26 +33,23 @@
             ).astype(out_ref.dtype)
 
 
-def norm(place, x, gain, slots):
+def norm(x, gain, slots):
     tokens, width = x.shape
-    rows = 32
+    rows = 64
     return pl.pallas_call(
         norm_kernel,
         out_shape=jax.ShapeDtypeStruct((slots, tokens, width // slots), BF16),
-        grid_spec=pltpu.PrefetchScalarGridSpec(
-            num_scalar_prefetch=1,
-            grid=(tokens // rows,),
-            in_specs=[
-                pl.BlockSpec((rows, width), lambda i, place: (i, 0)),
-                pl.BlockSpec((1, width), lambda i, place: (0, 0)),
-            ],
-            out_specs=pl.BlockSpec((slots, rows, width // slots), lambda i, place: (0, i, 0)),
-        ),
+        grid=(tokens // rows,),
+        in_specs=[
+            pl.BlockSpec((rows, width), lambda i: (i, 0)),
+            pl.BlockSpec((1, width), lambda i: (0, 0)),
+        ],
+        out_specs=pl.BlockSpec((slots, rows, width // slots), lambda i: (0, i, 0)),
         compiler_params=pltpu.CompilerParams(vmem_limit_bytes=NORM_VMEM_LIMIT),
         cost_estimate=pl.CostEstimate(
             flops=6 * tokens * width, bytes_accessed=4 * tokens * width, transcendentals=tokens
         ),
-    )(place, x, gain)
+    )(x, gain)
 
 
 def key_kernel(columns_ref, near_ref, far_ref, _, out_ref):
@@ -64,13 +61,13 @@
     out_ref[...] = terms.astype(out_ref.dtype)
 
 
-def key_products(columns, weights, before, dtype):
+def key_products(columns, weights, before):
     slots, tokens, width = columns.shape
     keys = weights[0].shape[1]
     in_vmem = pl.BlockSpec(memory_space=pltpu.VMEM)
     return pl.pallas_call(
         key_kernel,
-        out_shape=jax.ShapeDtypeStruct((slots * tokens, keys), dtype),
+        out_shape=jax.ShapeDtypeStruct((slots * tokens, keys), BF16),
         in_specs=[in_vmem] * 3 + [pl.BlockSpec(memory_space=pl.ANY)],
         out_specs=in_vmem,
         compiler_params=pltpu.CompilerParams(vmem_limit_bytes=VMEM_LIMIT),
@@ -180,15 +177,13 @@
     activations, norm_gain, key_weight, key_cotangent, fragment_local, outer_params, outer_momentum
 ):
     slots = lax.axis_size("y")
-    z, core = lax.axis_index("z"), lax.axis_index("core")
-    place = jnp.stack([z, core]).astype(jnp.int32)
     weight = key_weight[0]
     upstream = key_cotangent[0]
     part, keys = weight.shape
     tokens = upstream.shape[0]
 
     all_upstream = lax.all_gather(upstream, "y", axis=0, tiled=True)
-    hidden = norm(place, activations[0], norm_gain, slots)
+    hidden = norm(activations[0], norm_gain, slots)
     columns = lax.all_to_all(hidden, "y", 0, 0, tiled=True)
 
     near_weight = jnp.concatenate([weight, swap(weight, "z")], axis=0)
@@ -202,7 +197,7 @@
     new_momentum = 0.9 * outer_momentum + pseudo_grad
     new_params = outer_params - 0.7 * (pseudo_grad + 0.9 * new_momentum)
 
-    key_terms = key_products(columns, weights, new_params, BF16)
+    key_terms = key_products(columns, weights, new_params)
     key_out = lax.psum_scatter(key_terms, "y", scatter_dimension=0, tiled=True).astype(BF16)
 
     near, far = grad_products(columns, all_upstream, key_terms)

time: 139 us -> 137 us (0.986)
  the two profiles are of different devices: /device:TPU:2 before, /device:TPU:4 now
where the time goes in v5:
time: 137 us; the launch traced here: 136 us
  starting transfers between devices  57.1 us (42%)
  waiting for transfers between devices  48.3 us (35%)
  between operations  14.3 us (10%)
  Pallas kernels  11.4 us (8%)
  other arithmetic  2.69 us (2%)
  local copies, waits for them, and re-layouts  2.14 us (2%)
    ppermute x4, starting transfers between devices, swap(): return lax.ppermute(x, axis, [(0, 1), (1, 0)])  22.4 us
    all_to_all x1, waiting for transfers between devices, body(): columns = lax.all_to_all(hidden, 'y', 0, 0, tiled=True)  14.7 us
    all_to_all x1, starting transfers between devices, body(): lax.all_to_all(jnp.broadcast_to(terms[:1], (devices, 4 * part)), FSDP, 0,...  13.8 us
    ppermute x4, starting transfers between devices, halved(): received = lax.ppermute(sent, axis, [(i, i ^ bit) for i in range(size)])  13.6 us
    ppermute x4, waiting for transfers between devices, halved(): received = lax.ppermute(sent, axis, [(i, i ^ bit) for i in range(size)])  12.1 us
    reduce_scatter x1, waiting for transfers between devices, body(): lax.psum_scatter(key_terms, 'y', scatter_dimension=0, tiled=True)  8.45 us
    all_to_all x1, waiting for transfers between devices, body(): lax.all_to_all(jnp.broadcast_to(terms[:1], (devices, 4 * part)), FSDP, 0,...  7.82 us
    all_to_all x1, starting transfers between devices, body(): columns = lax.all_to_all(hidden, 'y', 0, 0, tiled=True)  7.23 us
  transfers between devices with their start and end apart: 12, of which 9 were waited for; matrix products, arithmetic and copies ran while one was open for 3% of the time, Pallas kernels for 4%

profile of v5, /device:TPU:4, one launch (start us, length us, event | category | flops | bytes accessed | tf_op | source)
XLA Modules:
  0.0 136.0 jit_solution(8891218049588327060)
XLA Ops:
  7.2 3.2 %shard_map.110 = bf16[8,128,1024]{2,1,0:T(8,128)(2,1)} custom-call(bf16[128,8192]{1,0:T(8,128)(2,1)} %bitcast.91, f32[1,8192]{1,0:T(1,128)} %gain_ref.1), custom_call_target="tpu_custom_call" | custom-call | flops 6291456 | bytes 4194304 | tf_op jit(solution)/shard_map/pallas_call | solution.py:39
  10.4 7.2 %all-to-all-start = ((bf16[8,128,1024]{2,1,0:T(8,128)(2,1)}), bf16[8,128,1024]{2,1,0:T(8,128)(2,1)S(1)}, u32[]{:S(2)}, u32[]{:S(2)}) async-start(bf16[8,128,1024]{2,1,0:T(8,128)(2,1)} %shard_map.110), calls=%async_computation | async-start | bytes 4194304 | tf_op jit(solution)/shard_map/all_to_all | solution.py:187
  17.7 4.3 %collective-permute-start.2 = (bf16[128,512]{1,0:T(8,128)(2,1)S(1)}, bf16[128,512]{1,0:T(8,128)(2,1)S(1)}, u32[]{:S(2)}, u32[]{:S(2)}) collective-permute-start(bf16[128,512]{1,0:T(8,128)(2,1)S(1)} %select_bitcast_fusion), channel_id=1, source_target_pairs={{0,256},{128,384},{256,0},{384,128},{1,257},{129,385},{257,1},{385... | collective-permute-start | bytes 393224 | tf_op jit(solution)/shard_map/ppermute | solution.py:172
  22.1 4.0 %collective-permute-done.2 = bf16[128,512]{1,0:T(8,128)(2,1)S(1)} collective-permute-done((bf16[128,512]{1,0:T(8,128)(2,1)S(1)}, bf16[128,512]{1,0:T(8,128)(2,1)S(1)}, u32[]{:S(2)}, u32[]{:S(2)}) %collective-permute-start.2) | collective-permute-done | bytes 131104 | tf_op jit(solution)/shard_map/ppermute | solution.py:172
  26.2 3.1 %collective-permute-start.3 = (f32[64,512]{1,0:T(8,128)S(1)}, f32[64,512]{1,0:T(8,128)S(1)}, u32[]{:S(2)}, u32[]{:S(2)}) collective-permute-start(f32[64,512]{1,0:T(8,128)S(1)} %slice_select_fusion), channel_id=1, source_target_pairs={{0,128},{128,0},{256,384},{384,256},{1,129},{129,1},{257,385},{385... | collective-permute-start | bytes 393224 | tf_op jit(solution)/shard_map/ppermute | solution.py:172
  29.3 10.9 %collective-permute-start = (bf16[256,512]{1,0:T(8,128)(2,1)S(1)}, bf16[256,512]{1,0:T(8,128)(2,1)S(1)}, u32[]{:S(2)}, u32[]{:S(2)}) collective-permute-start(bf16[256,512]{1,0:T(8,128)(2,1)S(1)} %bitcast.92), channel_id=1, source_target_pairs={{0,16},{16,0},{1,17},{17,1},{2,18},{18,2},{3,19},{19,3},{4,20},{20... | collective-permute-start | bytes 786440 | tf_op jit(solution)/shard_map/ppermute | solution.py:163
  40.3 4.3 %collective-permute-start.4 = (f32[32,512]{1,0:T(8,128)S(1)}, f32[32,512]{1,0:T(8,128)S(1)}, u32[]{:S(2)}, u32[]{:S(2)}) collective-permute-start(f32[32,512]{1,0:T(8,128)S(1)} %slice_select_fusion.1), channel_id=1, source_target_pairs={{0,64},{32,96},{64,0},{96,32},{1,65},{33,97},{65,1},{97,33},{2,66}... | collective-permute-start | bytes 196616 | tf_op jit(solution)/shard_map/ppermute | solution.py:172
  44.6 3.6 %collective-permute-done = bf16[256,512]{1,0:T(8,128)(2,1)S(1)} collective-permute-done((bf16[256,512]{1,0:T(8,128)(2,1)S(1)}, bf16[256,512]{1,0:T(8,128)(2,1)S(1)}, u32[]{:S(2)}, u32[]{:S(2)}) %collective-permute-start) | collective-permute-done | bytes 262176 | tf_op jit(solution)/shard_map/ppermute | solution.py:163
  48.3 1.9 %collective-permute-start.1 = (bf16[512,512]{1,0:T(8,128)(2,1)S(1)}, bf16[512,512]{1,0:T(8,128)(2,1)S(1)}, u32[]{:S(2)}, u32[]{:S(2)}) collective-permute-start(bf16[512,512]{1,0:T(8,128)(2,1)S(1)} %pad_maximum_fusion.near_ref.near_weight_ref), channel_id=1, source_target_pairs={{0,1},{1,0},{2,3},{3,2},{4,5},{5,4},{6,7},{7,6},{8,9},{9,8},{10,11... | collective-permute-start | bytes 1572872 | tf_op jit(solution)/shard_map/ppermute | solution.py:163
  50.2 4.2 %collective-permute-done.4 = f32[32,512]{1,0:T(8,128)S(1)} collective-permute-done((f32[32,512]{1,0:T(8,128)S(1)}, f32[32,512]{1,0:T(8,128)S(1)}, u32[]{:S(2)}, u32[]{:S(2)}) %collective-permute-start.4) | collective-permute-done | bytes 65568 | tf_op jit(solution)/shard_map/ppermute | solution.py:172
  54.5 1.9 %collective-permute-start.5 = (f32[16,512]{1,0:T(8,128)S(1)}, f32[16,512]{1,0:T(8,128)S(1)}, u32[]{:S(2)}, u32[]{:S(2)}) collective-permute-start(f32[16,512]{1,0:T(8,128)S(1)} %slice_select_fusion.2), channel_id=1, source_target_pairs={{0,32},{32,0},{64,96},{96,64},{1,33},{33,1},{65,97},{97,65},{2,34}... | collective-permute-start | bytes 98312 | tf_op jit(solution)/shard_map/ppermute | solution.py:172
  56.4 3.9 %collective-permute-done.5 = f32[16,512]{1,0:T(8,128)S(1)} collective-permute-done((f32[16,512]{1,0:T(8,128)S(1)}, f32[16,512]{1,0:T(8,128)S(1)}, u32[]{:S(2)}, u32[]{:S(2)}) %collective-permute-start.5) | collective-permute-done | bytes 32800 | tf_op jit(solution)/shard_map/ppermute | solution.py:172
  60.3 0.6 multiply_subtract_fusion
  60.9 14.7 %all-to-all-done.columns_ref = bf16[8,128,1024]{2,1,0:T(8,128)(2,1)S(1)} async-done(((bf16[8,128,1024]{2,1,0:T(8,128)(2,1)}), bf16[8,128,1024]{2,1,0:T(8,128)(2,1)S(1)}, u32[]{:S(2)}, u32[]{:S(2)}) %all-to-all-start) | async-done | bytes 2097184 | tf_op jit(solution)/shard_map/all_to_all | solution.py:187
  75.6 2.2 %shard_map.111._ = bf16[1024,512]{1,0:T(8,128)(2,1)} custom-call(bf16[8,128,1024]{2,1,0:T(8,128)(2,1)S(1)} %all-to-all-done.columns_ref, bf16[512,512]{1,0:T(8,128)(2,1)S(1)} %pad_maximum_fusion.near_ref.near_weight_ref, bf16[512,512]{1,0:T(8,128)(2,1)S(1)} %collective-permute-done.1.far_ref.far_weight_ref, f32[16,512]{1,0:T(8,128)S(1)} %get-tuple-element.15._), custom_call_target="tpu_custom_call" | custom-call | flops 1073741824 | bytes 5242880 | tf_op jit(solution)/shard_map/pallas_call | solution.py:68
  77.8 1.2 copy-done.1
  79.1 2.9 %shard_map.112 = (f32[512,512]{1,0:T(8,128)S(1)}, f32[512,512]{1,0:T(8,128)S(1)}) custom-call(bf16[8,128,1024]{2,1,0:T(8,128)(2,1)} %copy-done, bf16[1024,512]{1,0:T(8,128)(2,1)S(1)} %bitcast.90, bf16[1024,512]{1,0:T(8,128)(2,1)} %shard_map.111._), custom_call_target="tpu_custom_call" | custom-call | flops 1073741824 | bytes 6291456 | tf_op jit(solution)/shard_map/pallas_call | solution.py:98
  81.9 1.9 %collective-permute-start.6 = (f32[512,512]{1,0:T(8,128)S(1)}, f32[512,512]{1,0:T(8,128)}, u32[]{:S(2)}, u32[]{:S(2)}) collective-permute-start(f32[512,512]{1,0:T(8,128)S(1)} %get-tuple-element.11.far_ref), channel_id=1, source_target_pairs={{0,1},{1,0},{2,3},{3,2},{4,5},{5,4},{6,7},{7,6},{8,9},{9,8},{10,11... | collective-permute-start | bytes 3145736 | tf_op jit(solution)/shard_map/ppermute | solution.py:163
  83.9 1.7 %shard_map.113.terms_ref = f32[8,1024]{1,0:T(8,128)S(1)} custom-call(f32[512,512]{1,0:T(8,128)S(1)} %get-tuple-element.10.near_ref, f32[512,512]{1,0:T(8,128)S(1)} %get-tuple-element.11.far_ref, bf16[512,512]{1,0:T(8,128)(2,1)S(1)} %pad_maximum_fusion.near_ref.near_weight_ref, bf16[512,512]{1,0:T(8,128)(2,1)S(1)} %collective-permute-done.1.far_ref.far_weight_ref), custom_call_target="tpu_custom_call" | custom-call | flops 4194304 | bytes 4194304 | tf_op jit(solution)/shard_map/pallas_call | solution.py:127
  85.6 1.0 collective-permute-done.6.other_ref
  86.6 1.3 shard_map.114
  88.0 0.7 broadcast_in_dim.13
  88.7 13.8 %all-to-all-start.1 = ((f32[32,1,1024]{2,1,0:T(1,128)}), f32[32,1,1024]{2,1,0:T(1,128)S(1)}, u32[]{:S(2)}, u32[]{:S(2)}) async-start(f32[32,1,1024]{2,1,0:T(1,128)} %broadcast_in_dim.13), calls=%async_computation.2 | async-start | bytes 262144 | tf_op jit(solution)/shard_map/all_to_all | solution.py:209
  102.5 7.6 %collective-permute-start.7 = (bf16[256,512]{1,0:T(8,128)(2,1)S(1)}, bf16[256,512]{1,0:T(8,128)(2,1)S(1)}, u32[]{:S(2)}, u32[]{:S(2)}) collective-permute-start(bf16[256,512]{1,0:T(8,128)(2,1)S(1)} %get-tuple-element.13), channel_id=1, source_target_pairs={{0,16},{16,0},{1,17},{17,1},{2,18},{18,2},{3,19},{19,3},{4,20},{20... | collective-permute-start | bytes 786440 | tf_op jit(solution)/shard_map/ppermute | solution.py:163
  110.1 7.8 %all-to-all-done.1 = f32[32,1,1024]{2,1,0:T(1,128)S(1)} async-done(((f32[32,1,1024]{2,1,0:T(1,128)}), f32[32,1,1024]{2,1,0:T(1,128)S(1)}, u32[]{:S(2)}, u32[]{:S(2)}) %all-to-all-start.1) | async-done | bytes 131104 | tf_op jit(solution)/shard_map/all_to_all | solution.py:209
  118.0 0.3 reduce
  118.3 0.1 reshape.191
  118.4 0.1 fusion.11
  118.6 0.7 div.11
  119.3 0.6 collective-permute-done.7
  119.9 0.8 fusion
  120.7 8.4 %reduce-scatter.2.cloned.1.call-done = bf16[128,512]{1,0:T(8,128)(2,1)} async-done(((bf16[1024,512]{1,0:T(8,128)(2,1)}), bf16[128,512]{1,0:T(8,128)(2,1)}) %reduce-scatter.2.cloned.1.call-update) | async-done | bytes 131088 | tf_op jit(solution)/shard_map/reduce_scatter | solution.py:201
  (35 shorter events, 0.5 us)
Async XLA Ops:
  10.4 7.3 %copy-start.3 = (bf16[1,256,512]{2,1,0:T(8,128)(2,1)S(1)}, bf16[1,256,512]{2,1,0:T(8,128)(2,1)}, u32[]{:S(2)}) copy-start(bf16[1,256,512]{2,1,0:T(8,128)(2,1)} %param.11) | copy-start | bytes 786436
  10.4 18.9 %copy-start.4 = (bf16[1,256,512]{2,1,0:T(8,128)(2,1)S(1)}, bf16[1,256,512]{2,1,0:T(8,128)(2,1)}, u32[]{:S(2)}) copy-start(bf16[1,256,512]{2,1,0:T(8,128)(2,1)} %param.9) | copy-start | bytes 786436
  10.4 65.2 %all-to-all-start = ((bf16[8,128,1024]{2,1,0:T(8,128)(2,1)}), bf16[8,128,1024]{2,1,0:T(8,128)(2,1)S(1)}, u32[]{:S(2)}, u32[]{:S(2)}) async-start(bf16[8,128,1024]{2,1,0:T(8,128)(2,1)} %shard_map.110), calls=%async_computation | async-start | bytes 4194304 | tf_op jit(solution)/shard_map/all_to_all | solution.py:187
  17.6 42.6 %copy-start.6 = (f32[16,512]{1,0:T(8,128)S(1)}, f32[16,512]{1,0:T(8,128)}, u32[]{:S(2)}) copy-start(f32[16,512]{1,0:T(8,128)} %param.12) | copy-start | bytes 98308
  17.6 42.6 %copy-start.7 = (f32[16,512]{1,0:T(8,128)S(1)}, f32[16,512]{1,0:T(8,128)}, u32[]{:S(2)}) copy-start(f32[16,512]{1,0:T(8,128)} %param.13) | copy-start | bytes 98308
  17.7 60.2 %all-gather.3.cloned.1.call-start = ((), (), s32[]{:S(2)}) async-start(), calls=%async_computation.4 | async-start | bytes 1179648 | tf_op jit(solution)/shard_map/all_gather | solution.py:185
  17.7 8.4 %collective-permute-start.2 = (bf16[128,512]{1,0:T(8,128)(2,1)S(1)}, bf16[128,512]{1,0:T(8,128)(2,1)S(1)}, u32[]{:S(2)}, u32[]{:S(2)}) collective-permute-start(bf16[128,512]{1,0:T(8,128)(2,1)S(1)} %select_bitcast_fusion), channel_id=1, source_target_pairs={{0,256},{128,384},{256,0},{384,128},{1,257},{129,385},{257,1},{385... | collective-permute-start | bytes 393224 | tf_op jit(solution)/shard_map/ppermute | solution.py:172
  22.1 107.0 %reduce-scatter.2.cloned.1.call-start = ((), (), s32[]{:S(2)}) async-start(), calls=%async_computation.3 | async-start | bytes 1179648 | tf_op jit(solution)/shard_map/reduce_scatter | solution.py:201
  26.2 14.1 %collective-permute-start.3 = (f32[64,512]{1,0:T(8,128)S(1)}, f32[64,512]{1,0:T(8,128)S(1)}, u32[]{:S(2)}, u32[]{:S(2)}) collective-permute-start(f32[64,512]{1,0:T(8,128)S(1)} %slice_select_fusion), channel_id=1, source_target_pairs={{0,128},{128,0},{256,384},{384,256},{1,129},{129,1},{257,385},{385... | collective-permute-start | bytes 393224 | tf_op jit(solution)/shard_map/ppermute | solution.py:172
  29.3 18.9 %collective-permute-start = (bf16[256,512]{1,0:T(8,128)(2,1)S(1)}, bf16[256,512]{1,0:T(8,128)(2,1)S(1)}, u32[]{:S(2)}, u32[]{:S(2)}) collective-permute-start(bf16[256,512]{1,0:T(8,128)(2,1)S(1)} %bitcast.92), channel_id=1, source_target_pairs={{0,16},{16,0},{1,17},{17,1},{2,18},{18,2},{3,19},{19,3},{4,20},{20... | collective-permute-start | bytes 786440 | tf_op jit(solution)/shard_map/ppermute | solution.py:163
  40.3 14.1 %collective-permute-start.4 = (f32[32,512]{1,0:T(8,128)S(1)}, f32[32,512]{1,0:T(8,128)S(1)}, u32[]{:S(2)}, u32[]{:S(2)}) collective-permute-start(f32[32,512]{1,0:T(8,128)S(1)} %slice_select_fusion.1), channel_id=1, source_target_pairs={{0,64},{32,96},{64,0},{96,32},{1,65},{33,97},{65,1},{97,33},{2,66}... | collective-permute-start | bytes 196616 | tf_op jit(solution)/shard_map/ppermute | solution.py:172
  48.3 12.6 %collective-permute-start.1 = (bf16[512,512]{1,0:T(8,128)(2,1)S(1)}, bf16[512,512]{1,0:T(8,128)(2,1)S(1)}, u32[]{:S(2)}, u32[]{:S(2)}) collective-permute-start(bf16[512,512]{1,0:T(8,128)(2,1)S(1)} %pad_maximum_fusion.near_ref.near_weight_ref), channel_id=1, source_target_pairs={{0,1},{1,0},{2,3},{3,2},{4,5},{5,4},{6,7},{7,6},{8,9},{9,8},{10,11... | collective-permute-start | bytes 1572872 | tf_op jit(solution)/shard_map/ppermute | solution.py:163
  54.5 5.8 %collective-permute-start.5 = (f32[16,512]{1,0:T(8,128)S(1)}, f32[16,512]{1,0:T(8,128)S(1)}, u32[]{:S(2)}, u32[]{:S(2)}) collective-permute-start(f32[16,512]{1,0:T(8,128)S(1)} %slice_select_fusion.2), channel_id=1, source_target_pairs={{0,32},{32,0},{64,96},{96,64},{1,33},{33,1},{65,97},{97,65},{2,34}... | collective-permute-start | bytes 98312 | tf_op jit(solution)/shard_map/ppermute | solution.py:172
  60.9 16.9 %copy-start.2 = (f32[16,512]{1,0:T(8,128)}, f32[16,512]{1,0:T(8,128)S(1)}, u32[]{:S(2)}) copy-start(f32[16,512]{1,0:T(8,128)S(1)} %get-tuple-element.15._) | copy-start | bytes 98308
  75.6 2.3 %copy-start = (bf16[8,128,1024]{2,1,0:T(8,128)(2,1)}, bf16[8,128,1024]{2,1,0:T(8,128)(2,1)S(1)}, u32[]{:S(2)}) copy-start(bf16[8,128,1024]{2,1,0:T(8,128)(2,1)S(1)} %all-to-all-done.columns_ref) | copy-start | bytes 6291460
  77.8 1.2 copy-start.1
  81.9 4.7 %collective-permute-start.6 = (f32[512,512]{1,0:T(8,128)S(1)}, f32[512,512]{1,0:T(8,128)}, u32[]{:S(2)}, u32[]{:S(2)}) collective-permute-start(f32[512,512]{1,0:T(8,128)S(1)} %get-tuple-element.11.far_ref), channel_id=1, source_target_pairs={{0,1},{1,0},{2,3},{3,2},{4,5},{5,4},{6,7},{7,6},{8,9},{9,8},{10,11... | collective-permute-start | bytes 3145736 | tf_op jit(solution)/shard_map/ppermute | solution.py:163
  85.6 33.0 %copy-start.5 = (f32[1,8192]{1,0:T(1,128)S(1)}, f32[1,8192]{1,0:T(1,128)}, u32[]{:S(2)}) copy-start(f32[1,8192]{1,0:T(1,128)} %gain_ref.1) | copy-start | bytes 98308
  88.7 29.3 %all-to-all-start.1 = ((f32[32,1,1024]{2,1,0:T(1,128)}), f32[32,1,1024]{2,1,0:T(1,128)S(1)}, u32[]{:S(2)}, u32[]{:S(2)}) async-start(f32[32,1,1024]{2,1,0:T(1,128)} %broadcast_in_dim.13), calls=%async_computation.2 | async-start | bytes 262144 | tf_op jit(solution)/shard_map/all_to_all | solution.py:209
  102.5 17.4 %collective-permute-start.7 = (bf16[256,512]{1,0:T(8,128)(2,1)S(1)}, bf16[256,512]{1,0:T(8,128)(2,1)S(1)}, u32[]{:S(2)}, u32[]{:S(2)}) collective-permute-start(bf16[256,512]{1,0:T(8,128)(2,1)S(1)} %get-tuple-element.13), channel_id=1, source_target_pairs={{0,16},{16,0},{1,17},{17,1},{2,18},{18,2},{3,19},{19,3},{4,20},{20... | collective-permute-start | bytes 786440 | tf_op jit(solution)/shard_map/ppermute | solution.py:163
Sparse Core Ops, SparseCore 0:
  22.2 55.2 all-gather.2
  84.0 45.0 reduce-scatter.1

commit v6 on v5

--- a/solution.py
+++ b/solution.py
@@ -35,7 +35,7 @@
 
 def norm(x, gain, slots):
     tokens, width = x.shape
-    rows = 64
+    rows = 128
     return pl.pallas_call(
         norm_kernel,
         out_shape=jax.ShapeDtypeStruct((slots, tokens, width // slots), BF16),

time: 137 us -> 137 us (level)
  no operation moved by 1% of the time
where the time goes in v6:
time: 137 us
  starting transfers between devices  57.2 us (42%)
  waiting for transfers between devices  48.3 us (35%)
  between operations  14.3 us (10%)
  Pallas kernels  12.1 us (9%)
  other arithmetic  2.69 us (2%)
  local copies, waits for them, and re-layouts  2.14 us (2%)
    ppermute x4, starting transfers between devices, swap(): return lax.ppermute(x, axis, [(0, 1), (1, 0)])  22.4 us
    all_to_all x1, waiting for transfers between devices, body(): columns = lax.all_to_all(hidden, 'y', 0, 0, tiled=True)  14.6 us
    all_to_all x1, starting transfers between devices, body(): lax.all_to_all(jnp.broadcast_to(terms[:1], (devices, 4 * part)), FSDP, 0,...  13.9 us
    ppermute x4, starting transfers between devices, halved(): received = lax.ppermute(sent, axis, [(i, i ^ bit) for i in range(size)])  13.6 us
    ppermute x4, waiting for transfers between devices, halved(): received = lax.ppermute(sent, axis, [(i, i ^ bit) for i in range(size)])  12.1 us
    reduce_scatter x1, waiting for transfers between devices, body(): lax.psum_scatter(key_terms, 'y', scatter_dimension=0, tiled=True)  8.48 us
    all_to_all x1, waiting for transfers between devices, body(): lax.all_to_all(jnp.broadcast_to(terms[:1], (devices, 4 * part)), FSDP, 0,...  7.81 us
    all_to_all x1, starting transfers between devices, body(): columns = lax.all_to_all(hidden, 'y', 0, 0, tiled=True)  7.23 us
  transfers between devices with their start and end apart: 12, of which 9 were waited for; matrix products, arithmetic and copies ran while one was open for 3% of the time, Pallas kernels for 4%

profile of v6, /device:TPU:4, one launch (start us, length us, event | category | flops | bytes accessed | tf_op | source)
XLA Modules:
  0.0 136.7 jit_solution(16979496374826619476)
XLA Ops:
  7.2 3.9 %shard_map.110 = bf16[8,128,1024]{2,1,0:T(8,128)(2,1)} custom-call(bf16[128,8192]{1,0:T(8,128)(2,1)} %bitcast.91, f32[1,8192]{1,0:T(1,128)} %gain_ref.1), custom_call_target="tpu_custom_call" | custom-call | flops 6291456 | bytes 4194304 | tf_op jit(solution)/shard_map/pallas_call | solution.py:39
  11.1 7.2 %all-to-all-start = ((bf16[8,128,1024]{2,1,0:T(8,128)(2,1)}), bf16[8,128,1024]{2,1,0:T(8,128)(2,1)S(1)}, u32[]{:S(2)}, u32[]{:S(2)}) async-start(bf16[8,128,1024]{2,1,0:T(8,128)(2,1)} %shard_map.110), calls=%async_computation | async-start | bytes 4194304 | tf_op jit(solution)/shard_map/all_to_all | solution.py:187
  18.4 4.3 %collective-permute-start.2 = (bf16[128,512]{1,0:T(8,128)(2,1)S(1)}, bf16[128,512]{1,0:T(8,128)(2,1)S(1)}, u32[]{:S(2)}, u32[]{:S(2)}) collective-permute-start(bf16[128,512]{1,0:T(8,128)(2,1)S(1)} %select_bitcast_fusion), channel_id=1, source_target_pairs={{0,256},{128,384},{256,0},{384,128},{1,257},{129,385},{257,1},{385... | collective-permute-start | bytes 393224 | tf_op jit(solution)/shard_map/ppermute | solution.py:172
  22.8 4.0 %collective-permute-done.2 = bf16[128,512]{1,0:T(8,128)(2,1)S(1)} collective-permute-done((bf16[128,512]{1,0:T(8,128)(2,1)S(1)}, bf16[128,512]{1,0:T(8,128)(2,1)S(1)}, u32[]{:S(2)}, u32[]{:S(2)}) %collective-permute-start.2) | collective-permute-done | bytes 131104 | tf_op jit(solution)/shard_map/ppermute | solution.py:172
  26.9 3.1 %collective-permute-start.3 = (f32[64,512]{1,0:T(8,128)S(1)}, f32[64,512]{1,0:T(8,128)S(1)}, u32[]{:S(2)}, u32[]{:S(2)}) collective-permute-start(f32[64,512]{1,0:T(8,128)S(1)} %slice_select_fusion), channel_id=1, source_target_pairs={{0,128},{128,0},{256,384},{384,256},{1,129},{129,1},{257,385},{385... | collective-permute-start | bytes 393224 | tf_op jit(solution)/shard_map/ppermute | solution.py:172
  30.0 10.9 %collective-permute-start = (bf16[256,512]{1,0:T(8,128)(2,1)S(1)}, bf16[256,512]{1,0:T(8,128)(2,1)S(1)}, u32[]{:S(2)}, u32[]{:S(2)}) collective-permute-start(bf16[256,512]{1,0:T(8,128)(2,1)S(1)} %bitcast.92), channel_id=1, source_target_pairs={{0,16},{16,0},{1,17},{17,1},{2,18},{18,2},{3,19},{19,3},{4,20},{20... | collective-permute-start | bytes 786440 | tf_op jit(solution)/shard_map/ppermute | solution.py:163
  41.0 4.3 %collective-permute-start.4 = (f32[32,512]{1,0:T(8,128)S(1)}, f32[32,512]{1,0:T(8,128)S(1)}, u32[]{:S(2)}, u32[]{:S(2)}) collective-permute-start(f32[32,512]{1,0:T(8,128)S(1)} %slice_select_fusion.1), channel_id=1, source_target_pairs={{0,64},{32,96},{64,0},{96,32},{1,65},{33,97},{65,1},{97,33},{2,66}... | collective-permute-start | bytes 196616 | tf_op jit(solution)/shard_map/ppermute | solution.py:172
  45.3 3.6 %collective-permute-done = bf16[256,512]{1,0:T(8,128)(2,1)S(1)} collective-permute-done((bf16[256,512]{1,0:T(8,128)(2,1)S(1)}, bf16[256,512]{1,0:T(8,128)(2,1)S(1)}, u32[]{:S(2)}, u32[]{:S(2)}) %collective-permute-start) | collective-permute-done | bytes 262176 | tf_op jit(solution)/shard_map/ppermute | solution.py:163
  49.0 1.9 %collective-permute-start.1 = (bf16[512,512]{1,0:T(8,128)(2,1)S(1)}, bf16[512,512]{1,0:T(8,128)(2,1)S(1)}, u32[]{:S(2)}, u32[]{:S(2)}) collective-permute-start(bf16[512,512]{1,0:T(8,128)(2,1)S(1)} %pad_maximum_fusion.near_ref.near_weight_ref), channel_id=1, source_target_pairs={{0,1},{1,0},{2,3},{3,2},{4,5},{5,4},{6,7},{7,6},{8,9},{9,8},{10,11... | collective-permute-start | bytes 1572872 | tf_op jit(solution)/shard_map/ppermute | solution.py:163
  50.9 4.2 %collective-permute-done.4 = f32[32,512]{1,0:T(8,128)S(1)} collective-permute-done((f32[32,512]{1,0:T(8,128)S(1)}, f32[32,512]{1,0:T(8,128)S(1)}, u32[]{:S(2)}, u32[]{:S(2)}) %collective-permute-start.4) | collective-permute-done | bytes 65568 | tf_op jit(solution)/shard_map/ppermute | solution.py:172
  55.1 1.9 %collective-permute-start.5 = (f32[16,512]{1,0:T(8,128)S(1)}, f32[16,512]{1,0:T(8,128)S(1)}, u32[]{:S(2)}, u32[]{:S(2)}) collective-permute-start(f32[16,512]{1,0:T(8,128)S(1)} %slice_select_fusion.2), channel_id=1, source_target_pairs={{0,32},{32,0},{64,96},{96,64},{1,33},{33,1},{65,97},{97,65},{2,34}... | collective-permute-start | bytes 98312 | tf_op jit(solution)/shard_map/ppermute | solution.py:172
  57.1 3.9 %collective-permute-done.5 = f32[16,512]{1,0:T(8,128)S(1)} collective-permute-done((f32[16,512]{1,0:T(8,128)S(1)}, f32[16,512]{1,0:T(8,128)S(1)}, u32[]{:S(2)}, u32[]{:S(2)}) %collective-permute-start.5) | collective-permute-done | bytes 32800 | tf_op jit(solution)/shard_map/ppermute | solution.py:172
  61.0 0.6 multiply_subtract_fusion
  61.6 14.6 %all-to-all-done.columns_ref = bf16[8,128,1024]{2,1,0:T(8,128)(2,1)S(1)} async-done(((bf16[8,128,1024]{2,1,0:T(8,128)(2,1)}), bf16[8,128,1024]{2,1,0:T(8,128)(2,1)S(1)}, u32[]{:S(2)}, u32[]{:S(2)}) %all-to-all-start) | async-done | bytes 2097184 | tf_op jit(solution)/shard_map/all_to_all | solution.py:187
  76.2 2.2 %shard_map.111._ = bf16[1024,512]{1,0:T(8,128)(2,1)} custom-call(bf16[8,128,1024]{2,1,0:T(8,128)(2,1)S(1)} %all-to-all-done.columns_ref, bf16[512,512]{1,0:T(8,128)(2,1)S(1)} %pad_maximum_fusion.near_ref.near_weight_ref, bf16[512,512]{1,0:T(8,128)(2,1)S(1)} %collective-permute-done.1.far_ref.far_weight_ref, f32[16,512]{1,0:T(8,128)S(1)} %get-tuple-element.15._), custom_call_target="tpu_custom_call" | custom-call | flops 1073741824 | bytes 5242880 | tf_op jit(solution)/shard_map/pallas_call | solution.py:68
  78.5 1.2 copy-done.1
  79.7 2.9 %shard_map.112 = (f32[512,512]{1,0:T(8,128)S(1)}, f32[512,512]{1,0:T(8,128)S(1)}) custom-call(bf16[8,128,1024]{2,1,0:T(8,128)(2,1)} %copy-done, bf16[1024,512]{1,0:T(8,128)(2,1)S(1)} %bitcast.90, bf16[1024,512]{1,0:T(8,128)(2,1)} %shard_map.111._), custom_call_target="tpu_custom_call" | custom-call | flops 1073741824 | bytes 6291456 | tf_op jit(solution)/shard_map/pallas_call | solution.py:98
  82.6 1.9 %collective-permute-start.6 = (f32[512,512]{1,0:T(8,128)S(1)}, f32[512,512]{1,0:T(8,128)}, u32[]{:S(2)}, u32[]{:S(2)}) collective-permute-start(f32[512,512]{1,0:T(8,128)S(1)} %get-tuple-element.11.far_ref), channel_id=1, source_target_pairs={{0,1},{1,0},{2,3},{3,2},{4,5},{5,4},{6,7},{7,6},{8,9},{9,8},{10,11... | collective-permute-start | bytes 3145736 | tf_op jit(solution)/shard_map/ppermute | solution.py:163
  84.5 1.7 %shard_map.113.terms_ref = f32[8,1024]{1,0:T(8,128)S(1)} custom-call(f32[512,512]{1,0:T(8,128)S(1)} %get-tuple-element.10.near_ref, f32[512,512]{1,0:T(8,128)S(1)} %get-tuple-element.11.far_ref, bf16[512,512]{1,0:T(8,128)(2,1)S(1)} %pad_maximum_fusion.near_ref.near_weight_ref, bf16[512,512]{1,0:T(8,128)(2,1)S(1)} %collective-permute-done.1.far_ref.far_weight_ref), custom_call_target="tpu_custom_call" | custom-call | flops 4194304 | bytes 4194304 | tf_op jit(solution)/shard_map/pallas_call | solution.py:127
  86.3 1.0 collective-permute-done.6.other_ref
  87.3 1.3 shard_map.114
  88.6 0.7 broadcast_in_dim.13
  89.3 13.9 %all-to-all-start.1 = ((f32[32,1,1024]{2,1,0:T(1,128)}), f32[32,1,1024]{2,1,0:T(1,128)S(1)}, u32[]{:S(2)}, u32[]{:S(2)}) async-start(f32[32,1,1024]{2,1,0:T(1,128)} %broadcast_in_dim.13), calls=%async_computation.2 | async-start | bytes 262144 | tf_op jit(solution)/shard_map/all_to_all | solution.py:209
  103.2 7.6 %collective-permute-start.7 = (bf16[256,512]{1,0:T(8,128)(2,1)S(1)}, bf16[256,512]{1,0:T(8,128)(2,1)S(1)}, u32[]{:S(2)}, u32[]{:S(2)}) collective-permute-start(bf16[256,512]{1,0:T(8,128)(2,1)S(1)} %get-tuple-element.13), channel_id=1, source_target_pairs={{0,16},{16,0},{1,17},{17,1},{2,18},{18,2},{3,19},{19,3},{4,20},{20... | collective-permute-start | bytes 786440 | tf_op jit(solution)/shard_map/ppermute | solution.py:163
  110.9 7.8 %all-to-all-done.1 = f32[32,1,1024]{2,1,0:T(1,128)S(1)} async-done(((f32[32,1,1024]{2,1,0:T(1,128)}), f32[32,1,1024]{2,1,0:T(1,128)S(1)}, u32[]{:S(2)}, u32[]{:S(2)}) %all-to-all-start.1) | async-done | bytes 131104 | tf_op jit(solution)/shard_map/all_to_all | solution.py:209
  118.7 0.3 reduce
  119.0 0.1 reshape.191
  119.1 0.1 fusion.11
  119.3 0.7 div.11
  120.0 0.6 collective-permute-done.7
  120.6 0.8 fusion
  121.4 8.5 %reduce-scatter.2.cloned.1.call-done = bf16[128,512]{1,0:T(8,128)(2,1)} async-done(((bf16[1024,512]{1,0:T(8,128)(2,1)}), bf16[128,512]{1,0:T(8,128)(2,1)}) %reduce-scatter.2.cloned.1.call-update) | async-done | bytes 131088 | tf_op jit(solution)/shard_map/reduce_scatter | solution.py:201
  (35 shorter events, 0.5 us)
Async XLA Ops:
  11.1 7.3 %copy-start.3 = (bf16[1,256,512]{2,1,0:T(8,128)(2,1)S(1)}, bf16[1,256,512]{2,1,0:T(8,128)(2,1)}, u32[]{:S(2)}) copy-start(bf16[1,256,512]{2,1,0:T(8,128)(2,1)} %param.11) | copy-start | bytes 786436
  11.1 18.9 %copy-start.4 = (bf16[1,256,512]{2,1,0:T(8,128)(2,1)S(1)}, bf16[1,256,512]{2,1,0:T(8,128)(2,1)}, u32[]{:S(2)}) copy-start(bf16[1,256,512]{2,1,0:T(8,128)(2,1)} %param.9) | copy-start | bytes 786436
  11.1 65.1 %all-to-all-start = ((bf16[8,128,1024]{2,1,0:T(8,128)(2,1)}), bf16[8,128,1024]{2,1,0:T(8,128)(2,1)S(1)}, u32[]{:S(2)}, u32[]{:S(2)}) async-start(bf16[8,128,1024]{2,1,0:T(8,128)(2,1)} %shard_map.110), calls=%async_computation | async-start | bytes 4194304 | tf_op jit(solution)/shard_map/all_to_all | solution.py:187
  18.3 42.6 %copy-start.6 = (f32[16,512]{1,0:T(8,128)S(1)}, f32[16,512]{1,0:T(8,128)}, u32[]{:S(2)}) copy-start(f32[16,512]{1,0:T(8,128)} %param.12) | copy-start | bytes 98308
  18.3 42.6 %copy-start.7 = (f32[16,512]{1,0:T(8,128)S(1)}, f32[16,512]{1,0:T(8,128)}, u32[]{:S(2)}) copy-start(f32[16,512]{1,0:T(8,128)} %param.13) | copy-start | bytes 98308
  18.3 60.1 %all-gather.3.cloned.1.call-start = ((), (), s32[]{:S(2)}) async-start(), calls=%async_computation.4 | async-start | bytes 1179648 | tf_op jit(solution)/shard_map/all_gather | solution.py:185
  18.4 8.4 %collective-permute-start.2 = (bf16[128,512]{1,0:T(8,128)(2,1)S(1)}, bf16[128,512]{1,0:T(8,128)(2,1)S(1)}, u32[]{:S(2)}, u32[]{:S(2)}) collective-permute-start(bf16[128,512]{1,0:T(8,128)(2,1)S(1)} %select_bitcast_fusion), channel_id=1, source_target_pairs={{0,256},{128,384},{256,0},{384,128},{1,257},{129,385},{257,1},{385... | collective-permute-start | bytes 393224 | tf_op jit(solution)/shard_map/ppermute | solution.py:172
  22.8 107.1 %reduce-scatter.2.cloned.1.call-start = ((), (), s32[]{:S(2)}) async-start(), calls=%async_computation.3 | async-start | bytes 1179648 | tf_op jit(solution)/shard_map/reduce_scatter | solution.py:201
  26.9 14.1 %collective-permute-start.3 = (f32[64,512]{1,0:T(8,128)S(1)}, f32[64,512]{1,0:T(8,128)S(1)}, u32[]{:S(2)}, u32[]{:S(2)}) collective-permute-start(f32[64,512]{1,0:T(8,128)S(1)} %slice_select_fusion), channel_id=1, source_target_pairs={{0,128},{128,0},{256,384},{384,256},{1,129},{129,1},{257,385},{385... | collective-permute-start | bytes 393224 | tf_op jit(solution)/shard_map/ppermute | solution.py:172
  30.0 18.9 %collective-permute-start = (bf16[256,512]{1,0:T(8,128)(2,1)S(1)}, bf16[256,512]{1,0:T(8,128)(2,1)S(1)}, u32[]{:S(2)}, u32[]{:S(2)}) collective-permute-start(bf16[256,512]{1,0:T(8,128)(2,1)S(1)} %bitcast.92), channel_id=1, source_target_pairs={{0,16},{16,0},{1,17},{17,1},{2,18},{18,2},{3,19},{19,3},{4,20},{20... | collective-permute-start | bytes 786440 | tf_op jit(solution)/shard_map/ppermute | solution.py:163
  41.0 14.1 %collective-permute-start.4 = (f32[32,512]{1,0:T(8,128)S(1)}, f32[32,512]{1,0:T(8,128)S(1)}, u32[]{:S(2)}, u32[]{:S(2)}) collective-permute-start(f32[32,512]{1,0:T(8,128)S(1)} %slice_select_fusion.1), channel_id=1, source_target_pairs={{0,64},{32,96},{64,0},{96,32},{1,65},{33,97},{65,1},{97,33},{2,66}... | collective-permute-start | bytes 196616 | tf_op jit(solution)/shard_map/ppermute | solution.py:172
  49.0 12.6 %collective-permute-start.1 = (bf16[512,512]{1,0:T(8,128)(2,1)S(1)}, bf16[512,512]{1,0:T(8,128)(2,1)S(1)}, u32[]{:S(2)}, u32[]{:S(2)}) collective-permute-start(bf16[512,512]{1,0:T(8,128)(2,1)S(1)} %pad_maximum_fusion.near_ref.near_weight_ref), channel_id=1, source_target_pairs={{0,1},{1,0},{2,3},{3,2},{4,5},{5,4},{6,7},{7,6},{8,9},{9,8},{10,11... | collective-permute-start | bytes 1572872 | tf_op jit(solution)/shard_map/ppermute | solution.py:163
  55.1 5.8 %collective-permute-start.5 = (f32[16,512]{1,0:T(8,128)S(1)}, f32[16,512]{1,0:T(8,128)S(1)}, u32[]{:S(2)}, u32[]{:S(2)}) collective-permute-start(f32[16,512]{1,0:T(8,128)S(1)} %slice_select_fusion.2), channel_id=1, source_target_pairs={{0,32},{32,0},{64,96},{96,64},{1,33},{33,1},{65,97},{97,65},{2,34}... | collective-permute-start | bytes 98312 | tf_op jit(solution)/shard_map/ppermute | solution.py:172
  61.6 16.9 %copy-start.2 = (f32[16,512]{1,0:T(8,128)}, f32[16,512]{1,0:T(8,128)S(1)}, u32[]{:S(2)}) copy-start(f32[16,512]{1,0:T(8,128)S(1)} %get-tuple-element.15._) | copy-start | bytes 98308
  76.2 2.2 %copy-start = (bf16[8,128,1024]{2,1,0:T(8,128)(2,1)}, bf16[8,128,1024]{2,1,0:T(8,128)(2,1)S(1)}, u32[]{:S(2)}) copy-start(bf16[8,128,1024]{2,1,0:T(8,128)(2,1)S(1)} %all-to-all-done.columns_ref) | copy-start | bytes 6291460
  78.5 1.2 copy-start.1
  82.6 4.7 %collective-permute-start.6 = (f32[512,512]{1,0:T(8,128)S(1)}, f32[512,512]{1,0:T(8,128)}, u32[]{:S(2)}, u32[]{:S(2)}) collective-permute-start(f32[512,512]{1,0:T(8,128)S(1)} %get-tuple-element.11.far_ref), channel_id=1, source_target_pairs={{0,1},{1,0},{2,3},{3,2},{4,5},{5,4},{6,7},{7,6},{8,9},{9,8},{10,11... | collective-permute-start | bytes 3145736 | tf_op jit(solution)/shard_map/ppermute | solution.py:163
  86.3 33.0 %copy-start.5 = (f32[1,8192]{1,0:T(1,128)S(1)}, f32[1,8192]{1,0:T(1,128)}, u32[]{:S(2)}) copy-start(f32[1,8192]{1,0:T(1,128)} %gain_ref.1) | copy-start | bytes 98308
  89.3 29.3 %all-to-all-start.1 = ((f32[32,1,1024]{2,1,0:T(1,128)}), f32[32,1,1024]{2,1,0:T(1,128)S(1)}, u32[]{:S(2)}, u32[]{:S(2)}) async-start(f32[32,1,1024]{2,1,0:T(1,128)} %broadcast_in_dim.13), calls=%async_computation.2 | async-start | bytes 262144 | tf_op jit(solution)/shard_map/all_to_all | solution.py:209
  103.2 17.3 %collective-permute-start.7 = (bf16[256,512]{1,0:T(8,128)(2,1)S(1)}, bf16[256,512]{1,0:T(8,128)(2,1)S(1)}, u32[]{:S(2)}, u32[]{:S(2)}) collective-permute-start(bf16[256,512]{1,0:T(8,128)(2,1)S(1)} %get-tuple-element.13), channel_id=1, source_target_pairs={{0,16},{16,0},{1,17},{17,1},{2,18},{18,2},{3,19},{19,3},{4,20},{20... | collective-permute-start | bytes 786440 | tf_op jit(solution)/shard_map/ppermute | solution.py:163
Sparse Core Ops, SparseCore 0:
  22.9 55.2 all-gather.2
  84.7 45.1 reduce-scatter.1
